TPU v7x, 128 devices: a whole 4x4x4 slice. The times are simulated.
128 devices in a mesh: section: 4 (over x), group: 4 (over y_hi, core), head: 8 (over z, y_lo).
Axes of the slice: x: 4, y: 4 (y_hi: 2, y_lo: 2; y = y_hi * 2 + y_lo), z: 4, core: 2. Of those that a mesh axis runs over, the one named last changes fastest.
Arguments:
- queries: bfloat16 [4, 8, 128, 576], P('group', None, ('section', 'head')), may hold values from -84 to 84
- cache: bfloat16 [4, 8, 4096, 576], P('group', None, ('section', 'head')), may hold values from -6 to 6
- kept_length: int32 [4, 8], P('group'), may hold values from 1024 to 4096, as said below
- w_uv: bfloat16 [128, 512, 128], P(('section', 'head')), may hold values from -0.75 to 0.75
- w_out: bfloat16 [16384, 7168], P(('section', 'head')), may hold values from -0.09375 to 0.09375
- resid: bfloat16 [4, 8, 7168], P('group', 'section', 'head'), may hold values from -3 to 3
- picks: int32 [4, 8, 8], P('group', 'section'), may hold values from 0 to 15, all different within a row; in each aligned block of 2 rows (0 to 1, 2 to 3, ..., all dimensions but the last counted through in order) at most 2 rows name the same one
- pick_logits: float32 [4, 8, 8], P('group', 'section'), may hold values from -6 to 6
- w_gate: bfloat16 [16, 7168, 2048], P(('section', 'group'), 'head'), may hold values from -0.0625 to 0.0625
- w_up: bfloat16 [16, 7168, 2048], P(('section', 'group'), 'head'), may hold values from -0.0625 to 0.0625
- w_down: bfloat16 [16, 2048, 7168], P(('section', 'group'), None, 'head'), may hold values from -0.125 to 0.125
Outputs:
- out: bfloat16 [4, 8, 7168], P('group', 'section', 'head')
Inputs may be any that keep to these rules, and one draw needn't show every extreme that they name: Request j of group g keeps its first kept_length[g, j] positions; some request keeps all 4096. Each token picks 8 different experts; since each token's 8 picks differ, an expert receives at most 2 of the 2 tokens of one section index of a group.
All inputs are finite; a program needn't handle non-finite values.
Results may differ from a plain program's by a relative error of at most 0.012.
Values may be sent and summed in bfloat16 or wider, within the bound.
No kernel may reach another device: no remote copies, remote signals or barrier semaphores. Data moves between devices by JAX's collectives and lax.ppermute only.
A program may use at most 256 MiB of HBM per device.

v0:
```python
import functools

import jax
import jax.numpy as jnp
from jax import lax
from jax.experimental import pallas as pl
from jax.experimental.pallas import tpu as pltpu
from jax.sharding import PartitionSpec as P

LAT = 512
ROPE = 64
VDIM = 128
D = 7168

neg_fill = -1e30
norm_eps = 1e-06
route_scale = 2.5
f32 = jnp.float32
bf16 = jnp.bfloat16
SPLIT = ("section", "head")
VMEM = pl.BlockSpec(memory_space=pltpu.VMEM)
FAR = pl.BlockSpec(memory_space=pltpu.HBM)


def exchange(x, axes):
    return lax.all_to_all(x, axes, split_axis=0, concat_axis=0, tiled=True)


def contract(a, b, dims):
    return lax.dot_general(a, b, (dims, ((), ())), preferred_element_type=f32)


def in_lanes(x):
    high = x.astype(bf16).astype(f32)
    rest = x - high
    middle = rest.astype(bf16).astype(f32)
    lane = lax.broadcasted_iota(jnp.int32, (x.shape[0], 128), 1)
    zero = jnp.zeros((x.shape[0], 128), f32)
    low = jnp.where(lane == 2, rest - middle, zero)
    return jnp.where(lane == 0, high, jnp.where(lane == 1, middle, low))


def start_all(moves):
    for move in moves:
        move.start()


def wait_all(moves):
    for move in moves:
        move.wait()


def label_here():
    return 2 * (lax.axis_index("section") % 2) + (lax.axis_index("head") // 2) % 2


def prepare_kernel(
    n_section,
    n_head,
    queries_ref,
    cache_ref,
    length_ref,
    asked_ref,
    p0,
    p1,
    p2,
    p3,
    length,
    q,
    q_sem,
    sems,
):
    label = label_here()
    asked = pltpu.make_async_copy(queries_ref.at[0], q, q_sem)
    asked.start()
    moves = [
        pltpu.make_async_copy(cache_ref.at[label ^ d], p, sems.at[i])
        for i, (d, p) in enumerate(((2, p1), (1, p2), (3, p3), (0, p0)))
    ]
    moves.append(pltpu.make_async_copy(length_ref, length, sems.at[4]))
    start_all(moves)
    asked.wait()
    heads = q.shape[1]
    for which in range(4):
        rows = [q[2 * which + r].astype(f32) for r in range(2)]
        block = jnp.concatenate(rows, axis=0).astype(bf16)
        for s in range(which // 2, n_section, 2):
            for z in range(which % 2, n_head // 2, 2):
                for y in range(2):
                    asked_ref[s * n_head + 2 * z + y] = block
    wait_all(moves)


def attend_kernel(
    n_section,
    n_head,
    q_ref,
    length_ref,
    k0,
    k1,
    k2,
    k3,
    ahead_ref,
    out_ref,
):
    section = lax.axis_index("section")
    head = lax.axis_index("head")
    label = label_here()
    block = k0.shape[2]
    sources = (
        (section, head),
        ((section + n_section - 1) % n_section, head),
        (section, (head + n_head - 2) % n_head),
        ((section + 1) % n_section, (head + 2) % n_head),
    )
    rows = q_ref.shape[0]
    first = lax.broadcasted_iota(jnp.int32, (rows, 1), 0) % 8 < 4
    lane = lax.broadcasted_iota(jnp.int32, (1, block), 1)
    position = jnp.concatenate([(s * n_head + h) * block + lane for s, h in sources], axis=1)
    q = q_ref[...]
    pages = [jnp.concatenate([k[r] for k in (k0, k1, k2, k3)], axis=1) for r in range(2)]
    scores = [contract(q, page, ((1,), (0,))) for page in pages]
    scores = jnp.where(first, scores[0], scores[1]) * ((VDIM + ROPE) ** -0.5)
    length = length_ref[...]
    named = lax.broadcasted_iota(jnp.int32, length.shape, 1) - 2 * label
    limit = [jnp.sum(jnp.where(named == r, length, 0), axis=1, keepdims=True) for r in range(2)]
    limit = jnp.where(first, limit[0], limit[1])
    counted = position < limit
    top = jnp.max(jnp.where(counted, scores, neg_fill), axis=1, keepdims=True)
    weights = jnp.where(counted, jnp.exp(scores - top), 0.0)
    total = jnp.sum(weights, axis=1, keepdims=True)
    weights = weights.astype(bf16)
    outs = [contract(weights, page[:LAT], ((1,), (1,))) for page in pages]
    any_kept = total > 0
    safe = jnp.where(any_kept, total, 1.0)
    out_ref[:, :LAT] = (jnp.where(first, outs[0], outs[1]) / safe).astype(bf16)
    level = jnp.where(any_kept, top + jnp.log(safe), neg_fill)
    out_ref[:, LAT:] = in_lanes(level).astype(bf16)


def project_kernel(
    n_section, n_head, got_ref, uv_ref, out_w_ref, resid_ref, ahead_gate, ahead_up, term_ref
):
    reqs, width_dev = term_ref.shape[2:]
    got = got_ref[...].astype(f32).reshape(n_section * n_head, 8, LAT + 128)
    level = jnp.sum(got[:, :, LAT:], axis=2, keepdims=True)
    merged = []
    for label in range(4):
        parts = [
            (2 * a + label // 2) * n_head + 2 * (2 * b + label % 2) + c
            for a in range(n_section // 2)
            for b in range(n_head // 4)
            for c in range(2)
        ]
        top = functools.reduce(jnp.maximum, [level[d] for d in parts])
        share = [jnp.exp(level[d] - top) for d in parts]
        total = functools.reduce(jnp.add, share)
        mix = functools.reduce(jnp.add, [w * got[d, :, :LAT] for w, d in zip(share, parts)])
        merged.append(mix / total)
    latent = jnp.concatenate(merged, axis=0).astype(bf16)
    heads = uv_ref.shape[0]
    row = lax.broadcasted_iota(jnp.int32, (reqs, reqs * heads), 0)
    column = lax.broadcasted_iota(jnp.int32, (reqs, reqs * heads), 1)
    values = []
    for i in range(heads):
        pick = (column == heads * row + i).astype(f32).astype(bf16)
        own = contract(pick, latent, ((1,), (0,))).astype(bf16)
        values.append(contract(own, uv_ref[i], ((1,), (0,))))
    values = jnp.concatenate(values, axis=1).astype(bf16)
    row = lax.broadcasted_iota(jnp.int32, (reqs, width_dev), 0)
    resid = resid_ref[0].astype(f32)
    spread = jnp.where(row % 2 == 0, resid[0:1], resid[1:2])
    spread = jnp.where(row // 2 == lax.axis_index("section"), spread, 0.0)
    head = lax.axis_index("head")
    for k in range(n_head):
        columns = slice(k * width_dev, (k + 1) * width_dev)
        term = contract(values, out_w_ref[:, columns], ((1,), (0,)))
        term = (term + jnp.where(head == k, spread, 0.0)).astype(bf16)
        for s in range(n_section):
            term_ref[s, k] = term


def rows_kernel(terms_ref, hidden_ref):
    reqs, width_dev = hidden_ref.shape
    terms = terms_ref[...].astype(f32).reshape(-1, reqs, width_dev)
    hidden_ref[...] = jnp.sum(terms, axis=0).astype(bf16)


def weigh_kernel(hidden_ref, picks_ref, logits_ref, weight_ref, mine_ref):
    rows_dev, n_expert = weight_ref.shape
    affinity = jax.nn.sigmoid(logits_ref[0])
    share = route_scale * affinity / jnp.sum(affinity, axis=1, keepdims=True)
    expert = lax.broadcasted_iota(jnp.int32, (rows_dev, n_expert), 1)
    weight = jnp.zeros((rows_dev, n_expert), f32)
    picks = picks_ref[0]
    for k in range(picks.shape[1]):
        weight += jnp.where(picks[:, k : k + 1] == expert, share[:, k : k + 1], 0.0)
    weight_ref[...] = weight
    hidden = hidden_ref[...].astype(f32)
    section = lax.axis_index("section")
    total = jnp.zeros(mine_ref.shape, f32)
    for s in range(hidden.shape[0] // rows_dev):
        total += jnp.where(section == s, hidden[s * rows_dev : (s + 1) * rows_dev], 0.0)
    mine_ref[...] = total


def expert_in_kernel(r0, r1, r2, r3, gate_ref, up_ref, after_ref, both_ref):
    wide = jnp.concatenate([r[...].astype(f32) for r in (r0, r1, r2, r3)], axis=0)
    rows = wide.astype(bf16)
    squares = in_lanes(jnp.sum(wide * wide, axis=1, keepdims=True)).astype(bf16)
    n_head = both_ref.shape[0]
    ff = gate_ref.shape[2] // n_head
    for k in range(n_head):
        columns = slice(k * ff, (k + 1) * ff)
        both_ref[k, :, :ff] = contract(rows, gate_ref[0, :, columns], ((1,), (0,))).astype(bf16)
        both_ref[k, :, ff : 2 * ff] = contract(
            rows, up_ref[0, :, columns], ((1,), (0,))
        ).astype(bf16)
        both_ref[k, :, 2 * ff :] = squares


def act_kernel(both_ref, act_ref):
    both = jnp.sum(both_ref[...].astype(f32), axis=0)
    ff = act_ref.shape[2]
    squares = jnp.sum(both[:, 2 * ff :], axis=1, keepdims=True)
    factor = lax.rsqrt(squares / D + norm_eps)
    gate = both[:, :ff] * factor
    act = gate * jax.nn.sigmoid(gate) * (both[:, ff : 2 * ff] * factor)
    act = act.astype(bf16)
    for k in range(act_ref.shape[0]):
        act_ref[k] = act


def expert_out_kernel(n_section, n_group, act_ref, down_ref, served_ref):
    n_head, _, ff = act_ref.shape
    act = jnp.concatenate([act_ref[k] for k in range(n_head)], axis=1)
    total = contract(act, down_ref[0], ((1,), (0,)))
    group = lax.axis_index("group")
    rows_dev = served_ref.shape[1]
    for d in range(n_group):
        for s in range(n_section):
            start = (d * n_section + s) * rows_dev
            served_ref[s * n_group + (group ^ d)] = total[start : start + rows_dev].astype(bf16)


def finish_kernel(back_ref, weight_ref, mine_ref, out_ref):
    weight = weight_ref[...]
    total = mine_ref[...]
    for e in range(back_ref.shape[0]):
        total += weight[:, e : e + 1] * back_ref[e].astype(f32)
    out_ref[0] = total.astype(bf16)


def run(kernel, shapes, *args, far=(), scratch=(), limit=16):
    single = isinstance(shapes[0], int)
    args = [
        pltpu.with_memory_space_constraint(a, pltpu.HBM) if i in far else a
        for i, a in enumerate(args)
    ]
    shapes = [
        jax.ShapeDtypeStruct(shape, bf16) if isinstance(shape, tuple) else shape
        for shape in ([shapes] if single else shapes)
    ]
    return pl.pallas_call(
        kernel,
        out_shape=shapes[0] if single else shapes,
        in_specs=[FAR if i in far else VMEM for i in range(len(args))],
        out_specs=VMEM if single else [VMEM] * len(shapes),
        scratch_shapes=list(scratch),
        compiler_params=pltpu.CompilerParams(vmem_limit_bytes=limit * 1024 * 1024),
    )(*args)


def local(
    queries, cache, kept_length, w_uv, w_out, resid, picks, pick_logits, w_gate, w_up, w_down
):
    n_section = lax.axis_size("section")
    n_group = lax.axis_size("group")
    n_head = lax.axis_size("head")
    n_shard = n_section * n_head
    n_expert = n_section * n_group
    reqs, heads_dev, width = queries.shape[1:]
    rows_dev, width_dev = resid.shape[1:]

    block = cache.shape[2]
    pages = jnp.swapaxes(cache[0], 1, 2).reshape(4, 2, width, block)
    dma = pltpu.SemaphoreType.DMA

    def passed(part, ds, dz):
        pairs = [
            (
                s * n_head + h,
                (s + ds) % n_section * n_head + (h + 2 * dz) % n_head,
            )
            for s in range(n_section)
            for h in range(n_head)
        ]
        return lax.ppermute(part, SPLIT, pairs)

    asked, own, *parts, lengths = run(
        functools.partial(prepare_kernel, n_section, n_head),
        [(n_shard, 2 * heads_dev, width)]
        + [(2, width, block)] * 4
        + [jax.ShapeDtypeStruct(kept_length.shape, jnp.int32)],
        queries,
        pages,
        kept_length,
        far=(0, 1, 2),
        scratch=[pltpu.VMEM((reqs, heads_dev, width), bf16), dma(()), dma((5,))],
    )
    moved = [passed(part, *way) for part, way in zip(parts, ((1, 0), (0, 1), (-1, -1)))]
    q_all = exchange(asked.reshape(n_shard * 2 * heads_dev, width), SPLIT)
    sent = run(
        functools.partial(attend_kernel, n_section, n_head),
        (q_all.shape[0], LAT + 128),
        q_all,
        lengths,
        own,
        *moved,
        w_out,
        far=(6,),
    )
    got = exchange(sent, SPLIT)
    term = run(
        functools.partial(project_kernel, n_section, n_head),
        (n_section, n_head, reqs, width_dev),
        got,
        w_uv,
        w_out,
        resid,
        w_gate,
        w_up,
        far=(4, 5),
    )
    terms = exchange(term.reshape(n_shard * reqs, width_dev), SPLIT)
    hidden = run(rows_kernel, (reqs, width_dev), terms)

    def from_group(d):
        return lax.ppermute(hidden, "group", [(g, g ^ d) for g in range(n_group)])

    others = [from_group(d) for d in range(1, n_group)]

    weight, mine = run(
        weigh_kernel,
        [
            jax.ShapeDtypeStruct((rows_dev, n_expert), f32),
            jax.ShapeDtypeStruct((rows_dev, width_dev), f32),
        ],
        hidden,
        picks,
        pick_logits,
    )

    ff_dev = w_gate.shape[2] // n_head
    count = n_group * reqs
    both = run(
        expert_in_kernel,
        (n_head, count, 2 * ff_dev + 128),
        hidden,
        *others,
        w_gate,
        w_up,
        mine,
    )
    both = exchange(both, "head")
    act = run(act_kernel, (n_head, count, ff_dev), both)
    act = exchange(act, "head")
    served = run(
        functools.partial(expert_out_kernel, n_section, n_group),
        (n_expert, rows_dev, width_dev),
        act,
        w_down,
    )
    back = exchange(served, ("section", "group"))
    return run(finish_kernel, (1, rows_dev, width_dev), back, weight, mine)


def solution(mesh):
    return jax.shard_map(
        local,
        mesh=mesh,
        in_specs=(
            P("group", None, ("section", "head"), None),
            P("group", None, ("section", "head"), None),
            P("group", None),
            P(("section", "head"), None, None),
            P(("section", "head"), None),
            P("group", "section", "head"),
            P("group", "section", None),
            P("group", "section", None),
            P(("section", "group"), "head", None),
            P(("section", "group"), "head", None),
            P(("section", "group"), None, "head"),
        ),
        out_specs=P("group", "section", "head"),
        check_vma=False,
    )
```

profile of v0, /device:TPU:1, one launch (start us, length us, event | category | flops | bytes accessed | tf_op | source)
XLA Modules:
  0.0 95.8 jit_solution(2630615567256567421)
XLA Ops:
  0.0 1.3 %shard_map.109 = (bf16[32,8,576]{2,1,0:T(8,128)(2,1)S(1)}, bf16[2,576,128]{2,1,0:T(8,128)(2,1)S(1)}, bf16[2,576,128]{2,1,0:T(8,128)(2,1)S(1)}, bf16[2,576,128]{2...) custom-call(bf16[1,8,4,576]{3,2,1,0:T(4,128)(2,1)} %queries_ref.1, ...), custom_call_target="tpu_custom_call" | custom-call | tf_op jit(solution)/shard_map/pallas_call | solution.py:264
  1.3 2.1 %collective-permute-start = (bf16[2,576,128]{2,1,0:T(8,128)(2,1)S(1)}, bf16[2,576,128]{2,1,0:T(8,128)(2,1)S(1)}, u32[]{:S(2)}, u32[]{:S(2)}) collective-permute-start(bf16[2,576,128]{2,1,0:T(8,128)(2,1)S(1)} %get-tuple-element.16), channel_id=1, source_target_pairs={{0,32},{1,33},{2,34},{3,35},{4,36},{5,37},{6,38},{7,39},{32,64},{3... | collective-permute-start | bytes 884744 | tf_op jit(solution)/shard_map/ppermute | solution.py:298
  3.4 1.6 %collective-permute-start.1 = (bf16[2,576,128]{2,1,0:T(8,128)(2,1)S(1)}, bf16[2,576,128]{2,1,0:T(8,128)(2,1)S(1)}, u32[]{:S(2)}, u32[]{:S(2)}) collective-permute-start(bf16[2,576,128]{2,1,0:T(8,128)(2,1)S(1)} %get-tuple-element.17), channel_id=1, source_target_pairs={{0,2},{1,3},{2,4},{3,5},{4,6},{5,7},{6,0},{7,1},{32,34},{33,35},{3... | collective-permute-start | bytes 884744 | tf_op jit(solution)/shard_map/ppermute | solution.py:298
  5.1 3.3 %collective-permute-start.2 = (bf16[2,576,128]{2,1,0:T(8,128)(2,1)S(1)}, bf16[2,576,128]{2,1,0:T(8,128)(2,1)S(1)}, u32[]{:S(2)}, u32[]{:S(2)}) collective-permute-start(bf16[2,576,128]{2,1,0:T(8,128)(2,1)S(1)} %get-tuple-element.18), channel_id=1, source_target_pairs={{0,102},{1,103},{2,96},{3,97},{4,98},{5,99},{6,100},{7,101},{32,6}... | collective-permute-start | bytes 884744 | tf_op jit(solution)/shard_map/ppermute | solution.py:298
  8.4 13.6 %all_to_all.45 = bf16[32,8,576]{2,1,0:T(8,128)(2,1)S(1)} all-to-all(bf16[32,8,576]{2,1,0:T(8,128)(2,1)S(1)} %get-tuple-element.13), channel_id=1, replica_groups=mesh['section'=4,'group'=4,'head'=8] {'section','head'}, dimensions={0} | all-to-all | bytes 589824 | tf_op jit(solution)/shard_map/all_to_all | solution.py:26
  22.0 0.0 collective-permute-done.k1
  22.0 0.0 collective-permute-done.1.k2
  22.0 0.0 collective-permute-done.2.k3
  22.0 0.0 copy-start
  22.0 0.0 copy-start.4
  22.0 0.0 copy-start.5
  22.0 1.1 %shard_map.110 = bf16[256,640]{1,0:T(8,128)(2,1)S(1)} custom-call(bf16[256,576]{1,0:T(8,128)(2,1)S(1)} %bitcast.12, s32[1,8]{1,0:T(1,128)S(1)} %get-tuple-element.14.length_ref, bf16[2,576,128]{2,1,0:T(8,128)(2,1)S(1)} %get-tuple-element.15.k0, bf16[2,576,128]{2,1,0:T(8,128)(2,1)S(1)} %collective-permute-done.k1, ...), custom_call_target="tpu_custom_call" | custom-call | tf_op jit(solution)/shard_map/pallas_call | solution.py:264
  23.1 12.2 %all_to_all.46 = bf16[32,8,640]{2,1,0:T(8,128)(2,1)S(1)} all-to-all(bf16[32,8,640]{2,1,0:T(8,128)(2,1)S(1)} %bitcast.13), channel_id=1, replica_groups=mesh['section'=4,'group'=4,'head'=8] {'section','head'}, dimensions={0} | all-to-all | bytes 655360 | tf_op jit(solution)/shard_map/all_to_all | solution.py:26
  35.3 0.0 copy-done
  35.3 0.0 copy-done.4
  35.3 0.0 copy-done.5
  35.3 0.0 copy-start.6
  35.4 0.0 copy-start.7
  35.4 0.0 copy-start.1
  35.4 0.0 copy-start.2
  35.4 1.8 %shard_map.111 = bf16[4,8,8,896]{3,2,1,0:T(8,128)(2,1)S(1)} custom-call(bf16[256,640]{1,0:T(8,128)(2,1)S(1)} %bitcast.14, bf16[4,512,128]{2,1,0:T(8,128)(2,1)S(1)} %copy-done.4, bf16[512,7168]{1,0:T(8,128)(2,1)S(1)} %copy-done, bf16[1,2,896]{2,1,0:T(2,128)(2,1)S(1)} %copy-done.5, bf16[1,896,2048]{2,1,0:T(8,128)(2,1)} %gate_ref.1, bf16[1,896,2048]{2,1,0:T(8,128)(2,1)} %up_ref.1), custom_call_target="tpu_custom_call" | custom-call | tf_op jit(solution)/shard_map/pallas_call | solution.py:264
  37.2 13.1 %all_to_all.47 = bf16[32,8,896]{2,1,0:T(8,128)(2,1)S(1)} all-to-all(bf16[32,8,896]{2,1,0:T(8,128)(2,1)S(1)} %bitcast.11), channel_id=1, replica_groups=mesh['section'=4,'group'=4,'head'=8] {'section','head'}, dimensions={0} | all-to-all | bytes 917504 | tf_op jit(solution)/shard_map/all_to_all | solution.py:26
  50.2 0.1 shard_map.112.hidden_ref.r0
  50.3 7.8 %collective-permute-start.5 = (bf16[8,896]{1,0:T(8,128)(2,1)S(1)}, bf16[8,896]{1,0:T(8,128)(2,1)S(1)}, u32[]{:S(2)}, u32[]{:S(2)}) collective-permute-start(bf16[8,896]{1,0:T(8,128)(2,1)S(1)} %shard_map.112.hidden_ref.r0), channel_id=1, source_target_pairs={{0,24},{8,16},{16,8},{24,0},{1,25},{9,17},{17,9},{25,1},{2,26},{10... | collective-permute-start | bytes 43016 | tf_op jit(solution)/shard_map/ppermute | solution.py:339
  58.1 0.3 collective-permute-start.4
  58.5 0.1 collective-permute-start.3
  58.6 0.0 copy-done.6
  58.6 0.0 copy-done.7
  58.6 0.2 shard_map.113
  58.8 1.1 %collective-permute-done.5.r3 = bf16[8,896]{1,0:T(8,128)(2,1)S(1)} collective-permute-done((bf16[8,896]{1,0:T(8,128)(2,1)S(1)}, bf16[8,896]{1,0:T(8,128)(2,1)S(1)}, u32[]{:S(2)}, u32[]{:S(2)}) %collective-permute-start.5) | collective-permute-done | bytes 14368 | tf_op jit(solution)/shard_map/ppermute | solution.py:339
  59.9 2.3 %collective-permute-done.4.r2 = bf16[8,896]{1,0:T(8,128)(2,1)S(1)} collective-permute-done((bf16[8,896]{1,0:T(8,128)(2,1)S(1)}, bf16[8,896]{1,0:T(8,128)(2,1)S(1)}, u32[]{:S(2)}, u32[]{:S(2)}) %collective-permute-start.4) | collective-permute-done | bytes 14368 | tf_op jit(solution)/shard_map/ppermute | solution.py:339
  62.2 0.0 collective-permute-done.3.r1
  62.2 0.0 copy-done.1
  62.2 0.0 copy-done.2
  62.2 0.0 copy-start.3
  62.2 1.4 %shard_map.114 = bf16[8,32,640]{2,1,0:T(8,128)(2,1)S(1)} custom-call(bf16[8,896]{1,0:T(8,128)(2,1)S(1)} %shard_map.112.hidden_ref.r0, bf16[8,896]{1,0:T(8,128)(2,1)S(1)} %collective-permute-done.3.r1, bf16[8,896]{1,0:T(8,128)(2,1)S(1)} %collective-permute-done.4.r2, bf16[8,896]{1,0:T(8,128)(2,1)S(1)} %collective-permute-done.5.r3, ...), custom_call_target="tpu_custom_call" | custom-call | tf_op jit(solution)/shard_map/pallas_call | solution.py:264
  63.6 10.0 %all_to_all.48.both_ref = bf16[8,32,640]{2,1,0:T(8,128)(2,1)S(1)} all-to-all(bf16[8,32,640]{2,1,0:T(8,128)(2,1)S(1)} %shard_map.114), channel_id=1, replica_groups=mesh['section'=4,'group'=4,'head'=8] {'head'}, dimensions={0} | all-to-all | bytes 655360 | tf_op jit(solution)/shard_map/all_to_all | solution.py:26
  73.6 0.1 shard_map.115
  73.7 7.9 %all_to_all.49.act_ref = bf16[8,32,256]{2,1,0:T(8,128)(2,1)S(1)} all-to-all(bf16[8,32,256]{2,1,0:T(8,128)(2,1)S(1)} %shard_map.115), channel_id=1, replica_groups=mesh['section'=4,'group'=4,'head'=8] {'head'}, dimensions={0} | all-to-all | bytes 262144 | tf_op jit(solution)/shard_map/all_to_all | solution.py:26
  81.6 0.0 copy-done.3
  81.6 0.7 shard_map.116
  82.4 12.7 %all_to_all.50.back_ref = bf16[16,2,896]{2,1,0:T(2,128)(2,1)S(1)} all-to-all(bf16[16,2,896]{2,1,0:T(2,128)(2,1)S(1)} %shard_map.116), channel_id=1, replica_groups=mesh['section'=4,'group'=4,'head'=8] {'section','group'}, dimensions={0} | all-to-all | bytes 114688 | tf_op jit(solution)/shard_map/all_to_all | solution.py:26
  95.1 0.7 shard_map.117
Async XLA Ops:
  1.3 20.7 %collective-permute-start = (bf16[2,576,128]{2,1,0:T(8,128)(2,1)S(1)}, bf16[2,576,128]{2,1,0:T(8,128)(2,1)S(1)}, u32[]{:S(2)}, u32[]{:S(2)}) collective-permute-start(bf16[2,576,128]{2,1,0:T(8,128)(2,1)S(1)} %get-tuple-element.16), channel_id=1, source_target_pairs={{0,32},{1,33},{2,34},{3,35},{4,36},{5,37},{6,38},{7,39},{32,64},{3... | collective-permute-start | bytes 884744 | tf_op jit(solution)/shard_map/ppermute | solution.py:298
  3.4 18.6 %collective-permute-start.1 = (bf16[2,576,128]{2,1,0:T(8,128)(2,1)S(1)}, bf16[2,576,128]{2,1,0:T(8,128)(2,1)S(1)}, u32[]{:S(2)}, u32[]{:S(2)}) collective-permute-start(bf16[2,576,128]{2,1,0:T(8,128)(2,1)S(1)} %get-tuple-element.17), channel_id=1, source_target_pairs={{0,2},{1,3},{2,4},{3,5},{4,6},{5,7},{6,0},{7,1},{32,34},{33,35},{3... | collective-permute-start | bytes 884744 | tf_op jit(solution)/shard_map/ppermute | solution.py:298
  5.1 16.9 %collective-permute-start.2 = (bf16[2,576,128]{2,1,0:T(8,128)(2,1)S(1)}, bf16[2,576,128]{2,1,0:T(8,128)(2,1)S(1)}, u32[]{:S(2)}, u32[]{:S(2)}) collective-permute-start(bf16[2,576,128]{2,1,0:T(8,128)(2,1)S(1)} %get-tuple-element.18), channel_id=1, source_target_pairs={{0,102},{1,103},{2,96},{3,97},{4,98},{5,99},{6,100},{7,101},{32,6}... | collective-permute-start | bytes 884744 | tf_op jit(solution)/shard_map/ppermute | solution.py:298
  22.0 13.3 %copy-start = (bf16[512,7168]{1,0:T(8,128)(2,1)S(1)}, bf16[512,7168]{1,0:T(8,128)(2,1)}, u32[]{:S(2)}) copy-start(bf16[512,7168]{1,0:T(8,128)(2,1)} %out_w_ref.1) | copy-start | bytes 22020100
  22.0 13.3 %copy-start.4 = (bf16[4,512,128]{2,1,0:T(8,128)(2,1)S(1)}, bf16[4,512,128]{2,1,0:T(8,128)(2,1)}, u32[]{:S(2)}) copy-start(bf16[4,512,128]{2,1,0:T(8,128)(2,1)} %uv_ref.1) | copy-start | bytes 1572868
  22.0 13.3 %copy-start.5 = (bf16[1,2,896]{2,1,0:T(2,128)(2,1)S(1)}, bf16[1,2,896]{2,1,0:T(2,128)(2,1)}, u32[]{:S(2)}) copy-start(bf16[1,2,896]{2,1,0:T(2,128)(2,1)} %resid_ref.1) | copy-start | bytes 10756
  35.3 23.3 %copy-start.6 = (s32[1,2,8]{2,1,0:T(2,128)S(1)}, s32[1,2,8]{2,1,0:T(2,128)}, u32[]{:S(2)}) copy-start(s32[1,2,8]{2,1,0:T(2,128)} %picks_ref.1) | copy-start | bytes 196
  35.4 23.2 %copy-start.7 = (f32[1,2,8]{2,1,0:T(2,128)S(1)}, f32[1,2,8]{2,1,0:T(2,128)}, u32[]{:S(2)}) copy-start(f32[1,2,8]{2,1,0:T(2,128)} %logits_ref.1) | copy-start | bytes 196
  35.4 26.8 %copy-start.1 = (bf16[1,896,2048]{2,1,0:T(8,128)(2,1)S(1)}, bf16[1,896,2048]{2,1,0:T(8,128)(2,1)}, u32[]{:S(2)}) copy-start(bf16[1,896,2048]{2,1,0:T(8,128)(2,1)} %gate_ref.1) | copy-start | bytes 11010052
  35.4 26.8 %copy-start.2 = (bf16[1,896,2048]{2,1,0:T(8,128)(2,1)S(1)}, bf16[1,896,2048]{2,1,0:T(8,128)(2,1)}, u32[]{:S(2)}) copy-start(bf16[1,896,2048]{2,1,0:T(8,128)(2,1)} %up_ref.1) | copy-start | bytes 11010052
  50.3 9.6 %collective-permute-start.5 = (bf16[8,896]{1,0:T(8,128)(2,1)S(1)}, bf16[8,896]{1,0:T(8,128)(2,1)S(1)}, u32[]{:S(2)}, u32[]{:S(2)}) collective-permute-start(bf16[8,896]{1,0:T(8,128)(2,1)S(1)} %shard_map.112.hidden_ref.r0), channel_id=1, source_target_pairs={{0,24},{8,16},{16,8},{24,0},{1,25},{9,17},{17,9},{25,1},{2,26},{10... | collective-permute-start | bytes 43016 | tf_op jit(solution)/shard_map/ppermute | solution.py:339
  58.1 4.1 %collective-permute-start.4 = (bf16[8,896]{1,0:T(8,128)(2,1)S(1)}, bf16[8,896]{1,0:T(8,128)(2,1)S(1)}, u32[]{:S(2)}, u32[]{:S(2)}) collective-permute-start(bf16[8,896]{1,0:T(8,128)(2,1)S(1)} %shard_map.112.hidden_ref.r0), channel_id=1, source_target_pairs={{0,16},{8,24},{16,0},{24,8},{1,17},{9,25},{17,1},{25,9},{2,18},{10... | collective-permute-start | bytes 43016 | tf_op jit(solution)/shard_map/ppermute | solution.py:339
  58.5 3.7 %collective-permute-start.3 = (bf16[8,896]{1,0:T(8,128)(2,1)S(1)}, bf16[8,896]{1,0:T(8,128)(2,1)S(1)}, u32[]{:S(2)}, u32[]{:S(2)}) collective-permute-start(bf16[8,896]{1,0:T(8,128)(2,1)S(1)} %shard_map.112.hidden_ref.r0), channel_id=1, source_target_pairs={{0,8},{8,0},{16,24},{24,16},{1,9},{9,1},{17,25},{25,17},{2,10},{10... | collective-permute-start | bytes 43016 | tf_op jit(solution)/shard_map/ppermute | solution.py:339
  62.2 19.4 %copy-start.3 = (bf16[1,2048,896]{2,1,0:T(8,128)(2,1)S(1)}, bf16[1,2048,896]{2,1,0:T(8,128)(2,1)}, u32[]{:S(2)}) copy-start(bf16[1,2048,896]{2,1,0:T(8,128)(2,1)} %down_ref.1) | copy-start | bytes 11010052
where the time goes:
time: 96 us; the launch traced here: 95.8 us
  blocking collectives  69.5 us (72%)
  starting transfers between devices  15.3 us (16%)
  Pallas kernels  7.32 us (8%)
  waiting for transfers between devices  3.4 us (4%)
    all_to_all x6, blocking collectives, exchange(): return lax.all_to_all(x, axes, split_axis=0, concat_axis=0, tiled=True)  69.5 us
    ppermute x3, starting transfers between devices, from_group(): return lax.ppermute(hidden, 'group', [(g, g ^ d) for g in range(n_group)])  8.28 us
    pallas_call x9, Pallas kernels, run(): pl.pallas_call(kernel, out_shape=shapes[0] if single else shapes, in_spec...  7.32 us
    ppermute x3, starting transfers between devices, passed(): return lax.ppermute(part, SPLIT, pairs)  7.05 us
    ppermute x3, waiting for transfers between devices, from_group(): return lax.ppermute(hidden, 'group', [(g, g ^ d) for g in range(n_group)])  3.39 us
  transfers between devices with their start and end apart: 6, of which 2 were waited for; matrix products, arithmetic and copies ran while one was open for 0% of the time, Pallas kernels for 0%

commit v1 on v0

--- a/solution.py
+++ b/solution.py
@@ -207,26 +207,39 @@
 def expert_in_kernel(r0, r1, r2, r3, gate_ref, up_ref, after_ref, both_ref):
     wide = jnp.concatenate([r[...].astype(f32) for r in (r0, r1, r2, r3)], axis=0)
     rows = wide.astype(bf16)
-    squares = in_lanes(jnp.sum(wide * wide, axis=1, keepdims=True)).astype(bf16)
+    squares = jnp.sum(wide * wide, axis=1, keepdims=True)
+    squares = jnp.sum(jnp.where(diagonal(rows.shape[0]), squares, 0.0), axis=0, keepdims=True)
+    high = squares.astype(bf16).astype(f32)
+    middle = (squares - high).astype(bf16).astype(f32)
+    row = lax.broadcasted_iota(jnp.int32, (8, 128), 0)
+    low = jnp.where(row == 2, squares - high - middle, 0.0)
+    squares = jnp.where(row == 0, high, jnp.where(row == 1, middle, low))
     n_head = both_ref.shape[0]
     ff = gate_ref.shape[2] // n_head
     for k in range(n_head):
         columns = slice(k * ff, (k + 1) * ff)
-        both_ref[k, :, :ff] = contract(rows, gate_ref[0, :, columns], ((1,), (0,))).astype(bf16)
-        both_ref[k, :, ff : 2 * ff] = contract(
-            rows, up_ref[0, :, columns], ((1,), (0,))
-        ).astype(bf16)
-        both_ref[k, :, 2 * ff :] = squares
+        parts = []
+        for w in (gate_ref, up_ref):
+            sums = contract(rows, w[0, :, columns], ((1,), (0,)))
+            parts += [sums[:, c : c + 128] for c in range(0, ff, 128)]
+        both_ref[k] = jnp.concatenate(parts + [squares], axis=0).astype(bf16)
+
+
+def diagonal(rows):
+    row = lax.broadcasted_iota(jnp.int32, (rows, 128), 0)
+    return row == lax.broadcasted_iota(jnp.int32, (rows, 128), 1)
 
 
 def act_kernel(both_ref, act_ref):
     both = jnp.sum(both_ref[...].astype(f32), axis=0)
-    ff = act_ref.shape[2]
-    squares = jnp.sum(both[:, 2 * ff :], axis=1, keepdims=True)
+    count, ff = act_ref.shape[1:]
+    blocks = [both[i * count : (i + 1) * count] for i in range(2 * ff // 128)]
+    squares = jnp.sum(both[2 * ff // 128 * count :], axis=0, keepdims=True)
+    squares = jnp.sum(jnp.where(diagonal(count), squares, 0.0), axis=1, keepdims=True)
     factor = lax.rsqrt(squares / D + norm_eps)
-    gate = both[:, :ff] * factor
-    act = gate * jax.nn.sigmoid(gate) * (both[:, ff : 2 * ff] * factor)
-    act = act.astype(bf16)
+    gate = jnp.concatenate(blocks[: ff // 128], axis=1) * factor
+    up = jnp.concatenate(blocks[ff // 128 :], axis=1) * factor
+    act = (gate * jax.nn.sigmoid(gate) * up).astype(bf16)
     for k in range(act_ref.shape[0]):
         act_ref[k] = act
 
@@ -355,7 +368,7 @@
     count = n_group * reqs
     both = run(
         expert_in_kernel,
-        (n_head, count, 2 * ff_dev + 128),
+        (n_head, 2 * ff_dev // 128 * count + 8, 128),
         hidden,
         *others,
         w_gate,

time: 96 us -> 95.6 us (level)
  no operation moved by 1% of the time
where the time goes in v1:
time: 95.6 us; the launch traced here: 95.3 us
  blocking collectives  69.1 us (72%)
  starting transfers between devices  15.3 us (16%)
  Pallas kernels  7.32 us (8%)
  waiting for transfers between devices  3.4 us (4%)
    all_to_all x6, blocking collectives, exchange(): return lax.all_to_all(x, axes, split_axis=0, concat_axis=0, tiled=True)  69.1 us
    ppermute x3, starting transfers between devices, from_group(): return lax.ppermute(hidden, 'group', [(g, g ^ d) for g in range(n_group)])  8.28 us
    pallas_call x9, Pallas kernels, run(): pl.pallas_call(kernel, out_shape=shapes[0] if single else shapes, in_spec...  7.32 us
    ppermute x3, starting transfers between devices, passed(): return lax.ppermute(part, SPLIT, pairs)  7.05 us
    ppermute x3, waiting for transfers between devices, from_group(): return lax.ppermute(hidden, 'group', [(g, g ^ d) for g in range(n_group)])  3.39 us
  transfers between devices with their start and end apart: 6, of which 2 were waited for; matrix products, arithmetic and copies ran while one was open for 0% of the time, Pallas kernels for 0%

profile of v1, /device:TPU:1, one launch (start us, length us, event | category | flops | bytes accessed | tf_op | source)
XLA Modules:
  0.0 95.3 jit_solution(13427716779944176564)
XLA Ops:
  0.0 1.3 %shard_map.109 = (bf16[32,8,576]{2,1,0:T(8,128)(2,1)S(1)}, bf16[2,576,128]{2,1,0:T(8,128)(2,1)S(1)}, bf16[2,576,128]{2,1,0:T(8,128)(2,1)S(1)}, bf16[2,576,128]{2...) custom-call(bf16[1,8,4,576]{3,2,1,0:T(4,128)(2,1)} %queries_ref.1, ...), custom_call_target="tpu_custom_call" | custom-call | tf_op jit(solution)/shard_map/pallas_call | solution.py:277
  1.3 2.1 %collective-permute-start = (bf16[2,576,128]{2,1,0:T(8,128)(2,1)S(1)}, bf16[2,576,128]{2,1,0:T(8,128)(2,1)S(1)}, u32[]{:S(2)}, u32[]{:S(2)}) collective-permute-start(bf16[2,576,128]{2,1,0:T(8,128)(2,1)S(1)} %get-tuple-element.16), channel_id=1, source_target_pairs={{0,32},{1,33},{2,34},{3,35},{4,36},{5,37},{6,38},{7,39},{32,64},{3... | collective-permute-start | bytes 884744 | tf_op jit(solution)/shard_map/ppermute | solution.py:311
  3.4 1.6 %collective-permute-start.1 = (bf16[2,576,128]{2,1,0:T(8,128)(2,1)S(1)}, bf16[2,576,128]{2,1,0:T(8,128)(2,1)S(1)}, u32[]{:S(2)}, u32[]{:S(2)}) collective-permute-start(bf16[2,576,128]{2,1,0:T(8,128)(2,1)S(1)} %get-tuple-element.17), channel_id=1, source_target_pairs={{0,2},{1,3},{2,4},{3,5},{4,6},{5,7},{6,0},{7,1},{32,34},{33,35},{3... | collective-permute-start | bytes 884744 | tf_op jit(solution)/shard_map/ppermute | solution.py:311
  5.1 3.3 %collective-permute-start.2 = (bf16[2,576,128]{2,1,0:T(8,128)(2,1)S(1)}, bf16[2,576,128]{2,1,0:T(8,128)(2,1)S(1)}, u32[]{:S(2)}, u32[]{:S(2)}) collective-permute-start(bf16[2,576,128]{2,1,0:T(8,128)(2,1)S(1)} %get-tuple-element.18), channel_id=1, source_target_pairs={{0,102},{1,103},{2,96},{3,97},{4,98},{5,99},{6,100},{7,101},{32,6}... | collective-permute-start | bytes 884744 | tf_op jit(solution)/shard_map/ppermute | solution.py:311
  8.4 13.6 %all_to_all.45 = bf16[32,8,576]{2,1,0:T(8,128)(2,1)S(1)} all-to-all(bf16[32,8,576]{2,1,0:T(8,128)(2,1)S(1)} %get-tuple-element.13), channel_id=1, replica_groups=mesh['section'=4,'group'=4,'head'=8] {'section','head'}, dimensions={0} | all-to-all | bytes 589824 | tf_op jit(solution)/shard_map/all_to_all | solution.py:26
  22.0 0.0 collective-permute-done.k1
  22.0 0.0 collective-permute-done.1.k2
  22.0 0.0 collective-permute-done.2.k3
  22.0 0.0 copy-start
  22.0 0.0 copy-start.4
  22.0 0.0 copy-start.5
  22.0 1.1 %shard_map.110 = bf16[256,640]{1,0:T(8,128)(2,1)S(1)} custom-call(bf16[256,576]{1,0:T(8,128)(2,1)S(1)} %bitcast.12, s32[1,8]{1,0:T(1,128)S(1)} %get-tuple-element.14.length_ref, bf16[2,576,128]{2,1,0:T(8,128)(2,1)S(1)} %get-tuple-element.15.k0, bf16[2,576,128]{2,1,0:T(8,128)(2,1)S(1)} %collective-permute-done.k1, ...), custom_call_target="tpu_custom_call" | custom-call | tf_op jit(solution)/shard_map/pallas_call | solution.py:277
  23.1 12.2 %all_to_all.46 = bf16[32,8,640]{2,1,0:T(8,128)(2,1)S(1)} all-to-all(bf16[32,8,640]{2,1,0:T(8,128)(2,1)S(1)} %bitcast.13), channel_id=1, replica_groups=mesh['section'=4,'group'=4,'head'=8] {'section','head'}, dimensions={0} | all-to-all | bytes 655360 | tf_op jit(solution)/shard_map/all_to_all | solution.py:26
  35.3 0.0 copy-done
  35.3 0.0 copy-done.4
  35.3 0.0 copy-done.5
  35.3 0.0 copy-start.6
  35.4 0.0 copy-start.7
  35.4 0.0 copy-start.1
  35.4 0.0 copy-start.2
  35.4 1.8 %shard_map.111 = bf16[4,8,8,896]{3,2,1,0:T(8,128)(2,1)S(1)} custom-call(bf16[256,640]{1,0:T(8,128)(2,1)S(1)} %bitcast.14, bf16[4,512,128]{2,1,0:T(8,128)(2,1)S(1)} %copy-done.4, bf16[512,7168]{1,0:T(8,128)(2,1)S(1)} %copy-done, bf16[1,2,896]{2,1,0:T(2,128)(2,1)S(1)} %copy-done.5, bf16[1,896,2048]{2,1,0:T(8,128)(2,1)} %gate_ref.1, bf16[1,896,2048]{2,1,0:T(8,128)(2,1)} %up_ref.1), custom_call_target="tpu_custom_call" | custom-call | tf_op jit(solution)/shard_map/pallas_call | solution.py:277
  37.2 13.1 %all_to_all.47 = bf16[32,8,896]{2,1,0:T(8,128)(2,1)S(1)} all-to-all(bf16[32,8,896]{2,1,0:T(8,128)(2,1)S(1)} %bitcast.11), channel_id=1, replica_groups=mesh['section'=4,'group'=4,'head'=8] {'section','head'}, dimensions={0} | all-to-all | bytes 917504 | tf_op jit(solution)/shard_map/all_to_all | solution.py:26
  50.2 0.1 shard_map.112.hidden_ref.r0
  50.3 7.8 %collective-permute-start.5 = (bf16[8,896]{1,0:T(8,128)(2,1)S(1)}, bf16[8,896]{1,0:T(8,128)(2,1)S(1)}, u32[]{:S(2)}, u32[]{:S(2)}) collective-permute-start(bf16[8,896]{1,0:T(8,128)(2,1)S(1)} %shard_map.112.hidden_ref.r0), channel_id=1, source_target_pairs={{0,24},{8,16},{16,8},{24,0},{1,25},{9,17},{17,9},{25,1},{2,26},{10... | collective-permute-start | bytes 43016 | tf_op jit(solution)/shard_map/ppermute | solution.py:352
  58.1 0.3 collective-permute-start.4
  58.5 0.1 collective-permute-start.3
  58.6 0.0 copy-done.6
  58.6 0.0 copy-done.7
  58.6 0.2 shard_map.113
  58.8 1.1 %collective-permute-done.5.r3 = bf16[8,896]{1,0:T(8,128)(2,1)S(1)} collective-permute-done((bf16[8,896]{1,0:T(8,128)(2,1)S(1)}, bf16[8,896]{1,0:T(8,128)(2,1)S(1)}, u32[]{:S(2)}, u32[]{:S(2)}) %collective-permute-start.5) | collective-permute-done | bytes 14368 | tf_op jit(solution)/shard_map/ppermute | solution.py:352
  59.9 2.3 %collective-permute-done.4.r2 = bf16[8,896]{1,0:T(8,128)(2,1)S(1)} collective-permute-done((bf16[8,896]{1,0:T(8,128)(2,1)S(1)}, bf16[8,896]{1,0:T(8,128)(2,1)S(1)}, u32[]{:S(2)}, u32[]{:S(2)}) %collective-permute-start.4) | collective-permute-done | bytes 14368 | tf_op jit(solution)/shard_map/ppermute | solution.py:352
  62.2 0.0 collective-permute-done.3.r1
  62.2 0.0 copy-done.1
  62.2 0.0 copy-done.2
  62.2 0.0 copy-start.3
  62.2 1.4 %shard_map.114 = bf16[8,136,128]{2,1,0:T(8,128)(2,1)S(1)} custom-call(bf16[8,896]{1,0:T(8,128)(2,1)S(1)} %shard_map.112.hidden_ref.r0, bf16[8,896]{1,0:T(8,128)(2,1)S(1)} %collective-permute-done.3.r1, bf16[8,896]{1,0:T(8,128)(2,1)S(1)} %collective-permute-done.4.r2, bf16[8,896]{1,0:T(8,128)(2,1)S(1)} %collective-permute-done.5.r3, ...), custom_call_target="tpu_custom_call" | custom-call | tf_op jit(solution)/shard_map/pallas_call | solution.py:277
  63.6 9.6 %all_to_all.48.both_ref = bf16[8,136,128]{2,1,0:T(8,128)(2,1)S(1)} all-to-all(bf16[8,136,128]{2,1,0:T(8,128)(2,1)S(1)} %shard_map.114), channel_id=1, replica_groups=mesh['section'=4,'group'=4,'head'=8] {'head'}, dimensions={0} | all-to-all | bytes 557056 | tf_op jit(solution)/shard_map/all_to_all | solution.py:26
  73.2 0.1 shard_map.115
  73.3 7.9 %all_to_all.49.act_ref = bf16[8,32,256]{2,1,0:T(8,128)(2,1)S(1)} all-to-all(bf16[8,32,256]{2,1,0:T(8,128)(2,1)S(1)} %shard_map.115), channel_id=1, replica_groups=mesh['section'=4,'group'=4,'head'=8] {'head'}, dimensions={0} | all-to-all | bytes 262144 | tf_op jit(solution)/shard_map/all_to_all | solution.py:26
  81.3 0.0 copy-done.3
  81.3 0.7 shard_map.116
  82.0 12.6 %all_to_all.50.back_ref = bf16[16,2,896]{2,1,0:T(2,128)(2,1)S(1)} all-to-all(bf16[16,2,896]{2,1,0:T(2,128)(2,1)S(1)} %shard_map.116), channel_id=1, replica_groups=mesh['section'=4,'group'=4,'head'=8] {'section','group'}, dimensions={0} | all-to-all | bytes 114688 | tf_op jit(solution)/shard_map/all_to_all | solution.py:26
  94.6 0.7 shard_map.117
Async XLA Ops:
  1.3 20.7 %collective-permute-start = (bf16[2,576,128]{2,1,0:T(8,128)(2,1)S(1)}, bf16[2,576,128]{2,1,0:T(8,128)(2,1)S(1)}, u32[]{:S(2)}, u32[]{:S(2)}) collective-permute-start(bf16[2,576,128]{2,1,0:T(8,128)(2,1)S(1)} %get-tuple-element.16), channel_id=1, source_target_pairs={{0,32},{1,33},{2,34},{3,35},{4,36},{5,37},{6,38},{7,39},{32,64},{3... | collective-permute-start | bytes 884744 | tf_op jit(solution)/shard_map/ppermute | solution.py:311
  3.4 18.6 %collective-permute-start.1 = (bf16[2,576,128]{2,1,0:T(8,128)(2,1)S(1)}, bf16[2,576,128]{2,1,0:T(8,128)(2,1)S(1)}, u32[]{:S(2)}, u32[]{:S(2)}) collective-permute-start(bf16[2,576,128]{2,1,0:T(8,128)(2,1)S(1)} %get-tuple-element.17), channel_id=1, source_target_pairs={{0,2},{1,3},{2,4},{3,5},{4,6},{5,7},{6,0},{7,1},{32,34},{33,35},{3... | collective-permute-start | bytes 884744 | tf_op jit(solution)/shard_map/ppermute | solution.py:311
  5.1 16.9 %collective-permute-start.2 = (bf16[2,576,128]{2,1,0:T(8,128)(2,1)S(1)}, bf16[2,576,128]{2,1,0:T(8,128)(2,1)S(1)}, u32[]{:S(2)}, u32[]{:S(2)}) collective-permute-start(bf16[2,576,128]{2,1,0:T(8,128)(2,1)S(1)} %get-tuple-element.18), channel_id=1, source_target_pairs={{0,102},{1,103},{2,96},{3,97},{4,98},{5,99},{6,100},{7,101},{32,6}... | collective-permute-start | bytes 884744 | tf_op jit(solution)/shard_map/ppermute | solution.py:311
  22.0 13.3 %copy-start = (bf16[512,7168]{1,0:T(8,128)(2,1)S(1)}, bf16[512,7168]{1,0:T(8,128)(2,1)}, u32[]{:S(2)}) copy-start(bf16[512,7168]{1,0:T(8,128)(2,1)} %out_w_ref.1) | copy-start | bytes 22020100
  22.0 13.3 %copy-start.4 = (bf16[4,512,128]{2,1,0:T(8,128)(2,1)S(1)}, bf16[4,512,128]{2,1,0:T(8,128)(2,1)}, u32[]{:S(2)}) copy-start(bf16[4,512,128]{2,1,0:T(8,128)(2,1)} %uv_ref.1) | copy-start | bytes 1572868
  22.0 13.3 %copy-start.5 = (bf16[1,2,896]{2,1,0:T(2,128)(2,1)S(1)}, bf16[1,2,896]{2,1,0:T(2,128)(2,1)}, u32[]{:S(2)}) copy-start(bf16[1,2,896]{2,1,0:T(2,128)(2,1)} %resid_ref.1) | copy-start | bytes 10756
  35.3 23.3 %copy-start.6 = (s32[1,2,8]{2,1,0:T(2,128)S(1)}, s32[1,2,8]{2,1,0:T(2,128)}, u32[]{:S(2)}) copy-start(s32[1,2,8]{2,1,0:T(2,128)} %picks_ref.1) | copy-start | bytes 196
  35.4 23.2 %copy-start.7 = (f32[1,2,8]{2,1,0:T(2,128)S(1)}, f32[1,2,8]{2,1,0:T(2,128)}, u32[]{:S(2)}) copy-start(f32[1,2,8]{2,1,0:T(2,128)} %logits_ref.1) | copy-start | bytes 196
  35.4 26.8 %copy-start.1 = (bf16[1,896,2048]{2,1,0:T(8,128)(2,1)S(1)}, bf16[1,896,2048]{2,1,0:T(8,128)(2,1)}, u32[]{:S(2)}) copy-start(bf16[1,896,2048]{2,1,0:T(8,128)(2,1)} %gate_ref.1) | copy-start | bytes 11010052
  35.4 26.8 %copy-start.2 = (bf16[1,896,2048]{2,1,0:T(8,128)(2,1)S(1)}, bf16[1,896,2048]{2,1,0:T(8,128)(2,1)}, u32[]{:S(2)}) copy-start(bf16[1,896,2048]{2,1,0:T(8,128)(2,1)} %up_ref.1) | copy-start | bytes 11010052
  50.3 9.6 %collective-permute-start.5 = (bf16[8,896]{1,0:T(8,128)(2,1)S(1)}, bf16[8,896]{1,0:T(8,128)(2,1)S(1)}, u32[]{:S(2)}, u32[]{:S(2)}) collective-permute-start(bf16[8,896]{1,0:T(8,128)(2,1)S(1)} %shard_map.112.hidden_ref.r0), channel_id=1, source_target_pairs={{0,24},{8,16},{16,8},{24,0},{1,25},{9,17},{17,9},{25,1},{2,26},{10... | collective-permute-start | bytes 43016 | tf_op jit(solution)/shard_map/ppermute | solution.py:352
  58.1 4.1 %collective-permute-start.4 = (bf16[8,896]{1,0:T(8,128)(2,1)S(1)}, bf16[8,896]{1,0:T(8,128)(2,1)S(1)}, u32[]{:S(2)}, u32[]{:S(2)}) collective-permute-start(bf16[8,896]{1,0:T(8,128)(2,1)S(1)} %shard_map.112.hidden_ref.r0), channel_id=1, source_target_pairs={{0,16},{8,24},{16,0},{24,8},{1,17},{9,25},{17,1},{25,9},{2,18},{10... | collective-permute-start | bytes 43016 | tf_op jit(solution)/shard_map/ppermute | solution.py:352
  58.5 3.7 %collective-permute-start.3 = (bf16[8,896]{1,0:T(8,128)(2,1)S(1)}, bf16[8,896]{1,0:T(8,128)(2,1)S(1)}, u32[]{:S(2)}, u32[]{:S(2)}) collective-permute-start(bf16[8,896]{1,0:T(8,128)(2,1)S(1)} %shard_map.112.hidden_ref.r0), channel_id=1, source_target_pairs={{0,8},{8,0},{16,24},{24,16},{1,9},{9,1},{17,25},{25,17},{2,10},{10... | collective-permute-start | bytes 43016 | tf_op jit(solution)/shard_map/ppermute | solution.py:352
  62.2 19.1 %copy-start.3 = (bf16[1,2048,896]{2,1,0:T(8,128)(2,1)S(1)}, bf16[1,2048,896]{2,1,0:T(8,128)(2,1)}, u32[]{:S(2)}) copy-start(bf16[1,2048,896]{2,1,0:T(8,128)(2,1)} %down_ref.1) | copy-start | bytes 11010052

commit v2 on v1

--- a/solution.py
+++ b/solution.py
@@ -159,14 +159,15 @@
         merged.append(mix / total)
     latent = jnp.concatenate(merged, axis=0).astype(bf16)
     heads = uv_ref.shape[0]
+    maps = jnp.concatenate([uv_ref[i] for i in range(heads)], axis=1)
+    wide = contract(latent, maps, ((1,), (0,)))
+    row = lax.broadcasted_iota(jnp.int32, wide.shape, 0)
+    column = lax.broadcasted_iota(jnp.int32, wide.shape, 1)
+    wide = jnp.where(row % heads == column // VDIM, wide, 0.0).astype(bf16)
     row = lax.broadcasted_iota(jnp.int32, (reqs, reqs * heads), 0)
     column = lax.broadcasted_iota(jnp.int32, (reqs, reqs * heads), 1)
-    values = []
-    for i in range(heads):
-        pick = (column == heads * row + i).astype(f32).astype(bf16)
-        own = contract(pick, latent, ((1,), (0,))).astype(bf16)
-        values.append(contract(own, uv_ref[i], ((1,), (0,))))
-    values = jnp.concatenate(values, axis=1).astype(bf16)
+    gather = (column // heads == row).astype(f32).astype(bf16)
+    values = contract(gather, wide, ((1,), (0,))).astype(bf16)
     row = lax.broadcasted_iota(jnp.int32, (reqs, width_dev), 0)
     resid = resid_ref[0].astype(f32)
     spread = jnp.where(row % 2 == 0, resid[0:1], resid[1:2])

time: 95.6 us -> 95.3 us (level)
  no operation moved by 1% of the time
where the time goes in v2:
time: 95.3 us; the launch traced here: 95 us
  blocking collectives  69.1 us (73%)
  starting transfers between devices  15.3 us (16%)
  Pallas kernels  7 us (7%)
  waiting for transfers between devices  3.4 us (4%)
    all_to_all x6, blocking collectives, exchange(): return lax.all_to_all(x, axes, split_axis=0, concat_axis=0, tiled=True)  69.1 us
    ppermute x3, starting transfers between devices, from_group(): return lax.ppermute(hidden, 'group', [(g, g ^ d) for g in range(n_group)])  8.28 us
    ppermute x3, starting transfers between devices, passed(): return lax.ppermute(part, SPLIT, pairs)  7.05 us
    pallas_call x9, Pallas kernels, run(): pl.pallas_call(kernel, out_shape=shapes[0] if single else shapes, in_spec...  7 us
    ppermute x3, waiting for transfers between devices, from_group(): return lax.ppermute(hidden, 'group', [(g, g ^ d) for g in range(n_group)])  3.39 us
  transfers between devices with their start and end apart: 6, of which 2 were waited for; matrix products, arithmetic and copies ran while one was open for 0% of the time, Pallas kernels for 0%

profile of v2, /device:TPU:1, one launch (start us, length us, event | category | flops | bytes accessed | tf_op | source)
XLA Modules:
  0.0 95.0 jit_solution(2003588438844698120)
XLA Ops:
  0.0 1.3 %shard_map.109 = (bf16[32,8,576]{2,1,0:T(8,128)(2,1)S(1)}, bf16[2,576,128]{2,1,0:T(8,128)(2,1)S(1)}, bf16[2,576,128]{2,1,0:T(8,128)(2,1)S(1)}, bf16[2,576,128]{2...) custom-call(bf16[1,8,4,576]{3,2,1,0:T(4,128)(2,1)} %queries_ref.1, ...), custom_call_target="tpu_custom_call" | custom-call | tf_op jit(solution)/shard_map/pallas_call | solution.py:278
  1.3 2.1 %collective-permute-start = (bf16[2,576,128]{2,1,0:T(8,128)(2,1)S(1)}, bf16[2,576,128]{2,1,0:T(8,128)(2,1)S(1)}, u32[]{:S(2)}, u32[]{:S(2)}) collective-permute-start(bf16[2,576,128]{2,1,0:T(8,128)(2,1)S(1)} %get-tuple-element.16), channel_id=1, source_target_pairs={{0,32},{1,33},{2,34},{3,35},{4,36},{5,37},{6,38},{7,39},{32,64},{3... | collective-permute-start | bytes 884744 | tf_op jit(solution)/shard_map/ppermute | solution.py:312
  3.4 1.6 %collective-permute-start.1 = (bf16[2,576,128]{2,1,0:T(8,128)(2,1)S(1)}, bf16[2,576,128]{2,1,0:T(8,128)(2,1)S(1)}, u32[]{:S(2)}, u32[]{:S(2)}) collective-permute-start(bf16[2,576,128]{2,1,0:T(8,128)(2,1)S(1)} %get-tuple-element.17), channel_id=1, source_target_pairs={{0,2},{1,3},{2,4},{3,5},{4,6},{5,7},{6,0},{7,1},{32,34},{33,35},{3... | collective-permute-start | bytes 884744 | tf_op jit(solution)/shard_map/ppermute | solution.py:312
  5.1 3.3 %collective-permute-start.2 = (bf16[2,576,128]{2,1,0:T(8,128)(2,1)S(1)}, bf16[2,576,128]{2,1,0:T(8,128)(2,1)S(1)}, u32[]{:S(2)}, u32[]{:S(2)}) collective-permute-start(bf16[2,576,128]{2,1,0:T(8,128)(2,1)S(1)} %get-tuple-element.18), channel_id=1, source_target_pairs={{0,102},{1,103},{2,96},{3,97},{4,98},{5,99},{6,100},{7,101},{32,6}... | collective-permute-start | bytes 884744 | tf_op jit(solution)/shard_map/ppermute | solution.py:312
  8.4 13.6 %all_to_all.45 = bf16[32,8,576]{2,1,0:T(8,128)(2,1)S(1)} all-to-all(bf16[32,8,576]{2,1,0:T(8,128)(2,1)S(1)} %get-tuple-element.13), channel_id=1, replica_groups=mesh['section'=4,'group'=4,'head'=8] {'section','head'}, dimensions={0} | all-to-all | bytes 589824 | tf_op jit(solution)/shard_map/all_to_all | solution.py:26
  22.0 0.0 collective-permute-done.k1
  22.0 0.0 collective-permute-done.1.k2
  22.0 0.0 collective-permute-done.2.k3
  22.0 0.0 copy-start
  22.0 0.0 copy-start.4
  22.0 0.0 copy-start.5
  22.0 1.1 %shard_map.110 = bf16[256,640]{1,0:T(8,128)(2,1)S(1)} custom-call(bf16[256,576]{1,0:T(8,128)(2,1)S(1)} %bitcast.12, s32[1,8]{1,0:T(1,128)S(1)} %get-tuple-element.14.length_ref, bf16[2,576,128]{2,1,0:T(8,128)(2,1)S(1)} %get-tuple-element.15.k0, bf16[2,576,128]{2,1,0:T(8,128)(2,1)S(1)} %collective-permute-done.k1, ...), custom_call_target="tpu_custom_call" | custom-call | tf_op jit(solution)/shard_map/pallas_call | solution.py:278
  23.1 12.2 %all_to_all.46 = bf16[32,8,640]{2,1,0:T(8,128)(2,1)S(1)} all-to-all(bf16[32,8,640]{2,1,0:T(8,128)(2,1)S(1)} %bitcast.13), channel_id=1, replica_groups=mesh['section'=4,'group'=4,'head'=8] {'section','head'}, dimensions={0} | all-to-all | bytes 655360 | tf_op jit(solution)/shard_map/all_to_all | solution.py:26
  35.3 0.0 copy-done
  35.3 0.0 copy-done.4
  35.3 0.0 copy-done.5
  35.3 0.0 copy-start.6
  35.4 0.0 copy-start.7
  35.4 0.0 copy-start.1
  35.4 0.0 copy-start.2
  35.4 1.4 %shard_map.111 = bf16[4,8,8,896]{3,2,1,0:T(8,128)(2,1)S(1)} custom-call(bf16[256,640]{1,0:T(8,128)(2,1)S(1)} %bitcast.14, bf16[4,512,128]{2,1,0:T(8,128)(2,1)S(1)} %copy-done.4, bf16[512,7168]{1,0:T(8,128)(2,1)S(1)} %copy-done, bf16[1,2,896]{2,1,0:T(2,128)(2,1)S(1)} %copy-done.5, bf16[1,896,2048]{2,1,0:T(8,128)(2,1)} %gate_ref.1, bf16[1,896,2048]{2,1,0:T(8,128)(2,1)} %up_ref.1), custom_call_target="tpu_custom_call" | custom-call | tf_op jit(solution)/shard_map/pallas_call | solution.py:278
  36.8 13.1 %all_to_all.47 = bf16[32,8,896]{2,1,0:T(8,128)(2,1)S(1)} all-to-all(bf16[32,8,896]{2,1,0:T(8,128)(2,1)S(1)} %bitcast.11), channel_id=1, replica_groups=mesh['section'=4,'group'=4,'head'=8] {'section','head'}, dimensions={0} | all-to-all | bytes 917504 | tf_op jit(solution)/shard_map/all_to_all | solution.py:26
  49.9 0.1 shard_map.112.hidden_ref.r0
  50.0 7.8 %collective-permute-start.5 = (bf16[8,896]{1,0:T(8,128)(2,1)S(1)}, bf16[8,896]{1,0:T(8,128)(2,1)S(1)}, u32[]{:S(2)}, u32[]{:S(2)}) collective-permute-start(bf16[8,896]{1,0:T(8,128)(2,1)S(1)} %shard_map.112.hidden_ref.r0), channel_id=1, source_target_pairs={{0,24},{8,16},{16,8},{24,0},{1,25},{9,17},{17,9},{25,1},{2,26},{10... | collective-permute-start | bytes 43016 | tf_op jit(solution)/shard_map/ppermute | solution.py:353
  57.8 0.3 collective-permute-start.4
  58.1 0.1 collective-permute-start.3
  58.3 0.0 copy-done.6
  58.3 0.0 copy-done.7
  58.3 0.2 shard_map.113
  58.5 1.1 %collective-permute-done.5.r3 = bf16[8,896]{1,0:T(8,128)(2,1)S(1)} collective-permute-done((bf16[8,896]{1,0:T(8,128)(2,1)S(1)}, bf16[8,896]{1,0:T(8,128)(2,1)S(1)}, u32[]{:S(2)}, u32[]{:S(2)}) %collective-permute-start.5) | collective-permute-done | bytes 14368 | tf_op jit(solution)/shard_map/ppermute | solution.py:353
  59.6 2.3 %collective-permute-done.4.r2 = bf16[8,896]{1,0:T(8,128)(2,1)S(1)} collective-permute-done((bf16[8,896]{1,0:T(8,128)(2,1)S(1)}, bf16[8,896]{1,0:T(8,128)(2,1)S(1)}, u32[]{:S(2)}, u32[]{:S(2)}) %collective-permute-start.4) | collective-permute-done | bytes 14368 | tf_op jit(solution)/shard_map/ppermute | solution.py:353
  61.9 0.0 collective-permute-done.3.r1
  61.9 0.0 copy-done.1
  61.9 0.0 copy-done.2
  61.9 0.0 copy-start.3
  61.9 1.4 %shard_map.114 = bf16[8,136,128]{2,1,0:T(8,128)(2,1)S(1)} custom-call(bf16[8,896]{1,0:T(8,128)(2,1)S(1)} %shard_map.112.hidden_ref.r0, bf16[8,896]{1,0:T(8,128)(2,1)S(1)} %collective-permute-done.3.r1, bf16[8,896]{1,0:T(8,128)(2,1)S(1)} %collective-permute-done.4.r2, bf16[8,896]{1,0:T(8,128)(2,1)S(1)} %collective-permute-done.5.r3, ...), custom_call_target="tpu_custom_call" | custom-call | tf_op jit(solution)/shard_map/pallas_call | solution.py:278
  63.2 9.6 %all_to_all.48.both_ref = bf16[8,136,128]{2,1,0:T(8,128)(2,1)S(1)} all-to-all(bf16[8,136,128]{2,1,0:T(8,128)(2,1)S(1)} %shard_map.114), channel_id=1, replica_groups=mesh['section'=4,'group'=4,'head'=8] {'head'}, dimensions={0} | all-to-all | bytes 557056 | tf_op jit(solution)/shard_map/all_to_all | solution.py:26
  72.9 0.1 shard_map.115
  73.0 7.9 %all_to_all.49.act_ref = bf16[8,32,256]{2,1,0:T(8,128)(2,1)S(1)} all-to-all(bf16[8,32,256]{2,1,0:T(8,128)(2,1)S(1)} %shard_map.115), channel_id=1, replica_groups=mesh['section'=4,'group'=4,'head'=8] {'head'}, dimensions={0} | all-to-all | bytes 262144 | tf_op jit(solution)/shard_map/all_to_all | solution.py:26
  80.9 0.0 copy-done.3
  80.9 0.7 shard_map.116
  81.7 12.7 %all_to_all.50.back_ref = bf16[16,2,896]{2,1,0:T(2,128)(2,1)S(1)} all-to-all(bf16[16,2,896]{2,1,0:T(2,128)(2,1)S(1)} %shard_map.116), channel_id=1, replica_groups=mesh['section'=4,'group'=4,'head'=8] {'section','group'}, dimensions={0} | all-to-all | bytes 114688 | tf_op jit(solution)/shard_map/all_to_all | solution.py:26
  94.3 0.7 shard_map.117
Async XLA Ops:
  1.3 20.7 %collective-permute-start = (bf16[2,576,128]{2,1,0:T(8,128)(2,1)S(1)}, bf16[2,576,128]{2,1,0:T(8,128)(2,1)S(1)}, u32[]{:S(2)}, u32[]{:S(2)}) collective-permute-start(bf16[2,576,128]{2,1,0:T(8,128)(2,1)S(1)} %get-tuple-element.16), channel_id=1, source_target_pairs={{0,32},{1,33},{2,34},{3,35},{4,36},{5,37},{6,38},{7,39},{32,64},{3... | collective-permute-start | bytes 884744 | tf_op jit(solution)/shard_map/ppermute | solution.py:312
  3.4 18.6 %collective-permute-start.1 = (bf16[2,576,128]{2,1,0:T(8,128)(2,1)S(1)}, bf16[2,576,128]{2,1,0:T(8,128)(2,1)S(1)}, u32[]{:S(2)}, u32[]{:S(2)}) collective-permute-start(bf16[2,576,128]{2,1,0:T(8,128)(2,1)S(1)} %get-tuple-element.17), channel_id=1, source_target_pairs={{0,2},{1,3},{2,4},{3,5},{4,6},{5,7},{6,0},{7,1},{32,34},{33,35},{3... | collective-permute-start | bytes 884744 | tf_op jit(solution)/shard_map/ppermute | solution.py:312
  5.1 16.9 %collective-permute-start.2 = (bf16[2,576,128]{2,1,0:T(8,128)(2,1)S(1)}, bf16[2,576,128]{2,1,0:T(8,128)(2,1)S(1)}, u32[]{:S(2)}, u32[]{:S(2)}) collective-permute-start(bf16[2,576,128]{2,1,0:T(8,128)(2,1)S(1)} %get-tuple-element.18), channel_id=1, source_target_pairs={{0,102},{1,103},{2,96},{3,97},{4,98},{5,99},{6,100},{7,101},{32,6}... | collective-permute-start | bytes 884744 | tf_op jit(solution)/shard_map/ppermute | solution.py:312
  22.0 13.3 %copy-start = (bf16[512,7168]{1,0:T(8,128)(2,1)S(1)}, bf16[512,7168]{1,0:T(8,128)(2,1)}, u32[]{:S(2)}) copy-start(bf16[512,7168]{1,0:T(8,128)(2,1)} %out_w_ref.1) | copy-start | bytes 22020100
  22.0 13.3 %copy-start.4 = (bf16[4,512,128]{2,1,0:T(8,128)(2,1)S(1)}, bf16[4,512,128]{2,1,0:T(8,128)(2,1)}, u32[]{:S(2)}) copy-start(bf16[4,512,128]{2,1,0:T(8,128)(2,1)} %uv_ref.1) | copy-start | bytes 1572868
  22.0 13.3 %copy-start.5 = (bf16[1,2,896]{2,1,0:T(2,128)(2,1)S(1)}, bf16[1,2,896]{2,1,0:T(2,128)(2,1)}, u32[]{:S(2)}) copy-start(bf16[1,2,896]{2,1,0:T(2,128)(2,1)} %resid_ref.1) | copy-start | bytes 10756
  35.3 22.9 %copy-start.6 = (s32[1,2,8]{2,1,0:T(2,128)S(1)}, s32[1,2,8]{2,1,0:T(2,128)}, u32[]{:S(2)}) copy-start(s32[1,2,8]{2,1,0:T(2,128)} %picks_ref.1) | copy-start | bytes 196
  35.4 22.9 %copy-start.7 = (f32[1,2,8]{2,1,0:T(2,128)S(1)}, f32[1,2,8]{2,1,0:T(2,128)}, u32[]{:S(2)}) copy-start(f32[1,2,8]{2,1,0:T(2,128)} %logits_ref.1) | copy-start | bytes 196
  35.4 26.5 %copy-start.1 = (bf16[1,896,2048]{2,1,0:T(8,128)(2,1)S(1)}, bf16[1,896,2048]{2,1,0:T(8,128)(2,1)}, u32[]{:S(2)}) copy-start(bf16[1,896,2048]{2,1,0:T(8,128)(2,1)} %gate_ref.1) | copy-start | bytes 11010052
  35.4 26.5 %copy-start.2 = (bf16[1,896,2048]{2,1,0:T(8,128)(2,1)S(1)}, bf16[1,896,2048]{2,1,0:T(8,128)(2,1)}, u32[]{:S(2)}) copy-start(bf16[1,896,2048]{2,1,0:T(8,128)(2,1)} %up_ref.1) | copy-start | bytes 11010052
  50.0 9.6 %collective-permute-start.5 = (bf16[8,896]{1,0:T(8,128)(2,1)S(1)}, bf16[8,896]{1,0:T(8,128)(2,1)S(1)}, u32[]{:S(2)}, u32[]{:S(2)}) collective-permute-start(bf16[8,896]{1,0:T(8,128)(2,1)S(1)} %shard_map.112.hidden_ref.r0), channel_id=1, source_target_pairs={{0,24},{8,16},{16,8},{24,0},{1,25},{9,17},{17,9},{25,1},{2,26},{10... | collective-permute-start | bytes 43016 | tf_op jit(solution)/shard_map/ppermute | solution.py:353
  57.8 4.1 %collective-permute-start.4 = (bf16[8,896]{1,0:T(8,128)(2,1)S(1)}, bf16[8,896]{1,0:T(8,128)(2,1)S(1)}, u32[]{:S(2)}, u32[]{:S(2)}) collective-permute-start(bf16[8,896]{1,0:T(8,128)(2,1)S(1)} %shard_map.112.hidden_ref.r0), channel_id=1, source_target_pairs={{0,16},{8,24},{16,0},{24,8},{1,17},{9,25},{17,1},{25,9},{2,18},{10... | collective-permute-start | bytes 43016 | tf_op jit(solution)/shard_map/ppermute | solution.py:353
  58.1 3.7 %collective-permute-start.3 = (bf16[8,896]{1,0:T(8,128)(2,1)S(1)}, bf16[8,896]{1,0:T(8,128)(2,1)S(1)}, u32[]{:S(2)}, u32[]{:S(2)}) collective-permute-start(bf16[8,896]{1,0:T(8,128)(2,1)S(1)} %shard_map.112.hidden_ref.r0), channel_id=1, source_target_pairs={{0,8},{8,0},{16,24},{24,16},{1,9},{9,1},{17,25},{25,17},{2,10},{10... | collective-permute-start | bytes 43016 | tf_op jit(solution)/shard_map/ppermute | solution.py:353
  61.9 19.1 %copy-start.3 = (bf16[1,2048,896]{2,1,0:T(8,128)(2,1)S(1)}, bf16[1,2048,896]{2,1,0:T(8,128)(2,1)}, u32[]{:S(2)}) copy-start(bf16[1,2048,896]{2,1,0:T(8,128)(2,1)} %down_ref.1) | copy-start | bytes 11010052

commit v3 on v2

--- a/solution.py
+++ b/solution.py
@@ -113,29 +113,37 @@
         (section, (head + n_head - 2) % n_head),
         ((section + 1) % n_section, (head + 2) % n_head),
     )
-    rows = q_ref.shape[0]
-    first = lax.broadcasted_iota(jnp.int32, (rows, 1), 0) % 8 < 4
     lane = lax.broadcasted_iota(jnp.int32, (1, block), 1)
     position = jnp.concatenate([(s * n_head + h) * block + lane for s, h in sources], axis=1)
-    q = q_ref[...]
-    pages = [jnp.concatenate([k[r] for k in (k0, k1, k2, k3)], axis=1) for r in range(2)]
-    scores = [contract(q, page, ((1,), (0,))) for page in pages]
-    scores = jnp.where(first, scores[0], scores[1]) * ((VDIM + ROPE) ** -0.5)
     length = length_ref[...]
     named = lax.broadcasted_iota(jnp.int32, length.shape, 1) - 2 * label
-    limit = [jnp.sum(jnp.where(named == r, length, 0), axis=1, keepdims=True) for r in range(2)]
-    limit = jnp.where(first, limit[0], limit[1])
-    counted = position < limit
-    top = jnp.max(jnp.where(counted, scores, neg_fill), axis=1, keepdims=True)
-    weights = jnp.where(counted, jnp.exp(scores - top), 0.0)
-    total = jnp.sum(weights, axis=1, keepdims=True)
-    weights = weights.astype(bf16)
-    outs = [contract(weights, page[:LAT], ((1,), (1,))) for page in pages]
-    any_kept = total > 0
-    safe = jnp.where(any_kept, total, 1.0)
-    out_ref[:, :LAT] = (jnp.where(first, outs[0], outs[1]) / safe).astype(bf16)
-    level = jnp.where(any_kept, top + jnp.log(safe), neg_fill)
-    out_ref[:, LAT:] = in_lanes(level).astype(bf16)
+    asked = q_ref[...].astype(f32).reshape(-1, 2, 8, q_ref.shape[1])
+    asked = by_half(asked[:, 0], asked[:, 1])
+    outs = []
+    for r in range(2):
+        page = jnp.concatenate([k[r] for k in (k0, k1, k2, k3)], axis=1)
+        q = asked[r].reshape(-1, q_ref.shape[1]).astype(bf16)
+        scores = contract(q, page, ((1,), (0,))) * ((VDIM + ROPE) ** -0.5)
+        limit = jnp.sum(jnp.where(named == r, length, 0), axis=1, keepdims=True)
+        counted = position < limit
+        top = jnp.max(jnp.where(counted, scores, neg_fill), axis=1, keepdims=True)
+        weights = jnp.where(counted, jnp.exp(scores - top), 0.0)
+        total = jnp.sum(weights, axis=1, keepdims=True)
+        out = contract(weights.astype(bf16), page[:LAT], ((1,), (1,)))
+        any_kept = total > 0
+        safe = jnp.where(any_kept, total, 1.0)
+        level = in_lanes(jnp.where(any_kept, top + jnp.log(safe), neg_fill))
+        outs.append(jnp.concatenate([out / safe, level], axis=1).reshape(-1, 8, LAT + 128))
+    sent = jnp.stack(by_half(*outs), axis=1)
+    out_ref[...] = sent.reshape(out_ref.shape).astype(bf16)
+
+
+def by_half(first, second):
+    upper = lax.broadcasted_iota(jnp.int32, first.shape, 1) < 4
+    return (
+        jnp.where(upper, first, pltpu.roll(second, 4, axis=1)),
+        jnp.where(upper, pltpu.roll(first, 4, axis=1), second),
+    )
 
 
 def project_kernel(
@@ -173,12 +181,14 @@
     spread = jnp.where(row % 2 == 0, resid[0:1], resid[1:2])
     spread = jnp.where(row // 2 == lax.axis_index("section"), spread, 0.0)
     head = lax.axis_index("head")
-    for k in range(n_head):
-        columns = slice(k * width_dev, (k + 1) * width_dev)
-        term = contract(values, out_w_ref[:, columns], ((1,), (0,)))
-        term = (term + jnp.where(head == k, spread, 0.0)).astype(bf16)
-        for s in range(n_section):
-            term_ref[s, k] = term
+    for k in range(0, n_head, 2):
+        columns = slice(k * width_dev, (k + 2) * width_dev)
+        pair = contract(values, out_w_ref[:, columns], ((1,), (0,)))
+        for d in range(2):
+            term = pair[:, d * width_dev : (d + 1) * width_dev]
+            term = (term + jnp.where(head == k + d, spread, 0.0)).astype(bf16)
+            for s in range(n_section):
+                term_ref[s, k + d] = term
 
 
 def rows_kernel(terms_ref, hidden_ref):

time: 95.3 us -> 95.3 us (level)
  no operation moved by 1% of the time
where the time goes in v3:
time: 95.3 us; the launch traced here: 95 us
  blocking collectives  69.1 us (73%)
  starting transfers between devices  15.3 us (16%)
  Pallas kernels  6.95 us (7%)
  waiting for transfers between devices  3.4 us (4%)
    all_to_all x6, blocking collectives, exchange(): return lax.all_to_all(x, axes, split_axis=0, concat_axis=0, tiled=True)  69.1 us
    ppermute x3, starting transfers between devices, from_group(): return lax.ppermute(hidden, 'group', [(g, g ^ d) for g in range(n_group)])  8.28 us
    ppermute x3, starting transfers between devices, passed(): return lax.ppermute(part, SPLIT, pairs)  7.05 us
    pallas_call x9, Pallas kernels, run(): pl.pallas_call(kernel, out_shape=shapes[0] if single else shapes, in_spec...  6.95 us
    ppermute x3, waiting for transfers between devices, from_group(): return lax.ppermute(hidden, 'group', [(g, g ^ d) for g in range(n_group)])  3.39 us
  transfers between devices with their start and end apart: 6, of which 2 were waited for; matrix products, arithmetic and copies ran while one was open for 0% of the time, Pallas kernels for 0%

profile of v3, /device:TPU:1, one launch (start us, length us, event | category | flops | bytes accessed | tf_op | source)
XLA Modules:
  0.0 95.0 jit_solution(1607761617996191301)
XLA Ops:
  0.0 1.3 %shard_map.109 = (bf16[32,8,576]{2,1,0:T(8,128)(2,1)S(1)}, bf16[2,576,128]{2,1,0:T(8,128)(2,1)S(1)}, bf16[2,576,128]{2,1,0:T(8,128)(2,1)S(1)}, bf16[2,576,128]{2...) custom-call(bf16[1,8,4,576]{3,2,1,0:T(4,128)(2,1)} %queries_ref.1, ...), custom_call_target="tpu_custom_call" | custom-call | tf_op jit(solution)/shard_map/pallas_call | solution.py:288
  1.3 2.1 %collective-permute-start = (bf16[2,576,128]{2,1,0:T(8,128)(2,1)S(1)}, bf16[2,576,128]{2,1,0:T(8,128)(2,1)S(1)}, u32[]{:S(2)}, u32[]{:S(2)}) collective-permute-start(bf16[2,576,128]{2,1,0:T(8,128)(2,1)S(1)} %get-tuple-element.16), channel_id=1, source_target_pairs={{0,32},{1,33},{2,34},{3,35},{4,36},{5,37},{6,38},{7,39},{32,64},{3... | collective-permute-start | bytes 884744 | tf_op jit(solution)/shard_map/ppermute | solution.py:322
  3.4 1.6 %collective-permute-start.1 = (bf16[2,576,128]{2,1,0:T(8,128)(2,1)S(1)}, bf16[2,576,128]{2,1,0:T(8,128)(2,1)S(1)}, u32[]{:S(2)}, u32[]{:S(2)}) collective-permute-start(bf16[2,576,128]{2,1,0:T(8,128)(2,1)S(1)} %get-tuple-element.17), channel_id=1, source_target_pairs={{0,2},{1,3},{2,4},{3,5},{4,6},{5,7},{6,0},{7,1},{32,34},{33,35},{3... | collective-permute-start | bytes 884744 | tf_op jit(solution)/shard_map/ppermute | solution.py:322
  5.1 3.3 %collective-permute-start.2 = (bf16[2,576,128]{2,1,0:T(8,128)(2,1)S(1)}, bf16[2,576,128]{2,1,0:T(8,128)(2,1)S(1)}, u32[]{:S(2)}, u32[]{:S(2)}) collective-permute-start(bf16[2,576,128]{2,1,0:T(8,128)(2,1)S(1)} %get-tuple-element.18), channel_id=1, source_target_pairs={{0,102},{1,103},{2,96},{3,97},{4,98},{5,99},{6,100},{7,101},{32,6}... | collective-permute-start | bytes 884744 | tf_op jit(solution)/shard_map/ppermute | solution.py:322
  8.4 13.6 %all_to_all.45 = bf16[32,8,576]{2,1,0:T(8,128)(2,1)S(1)} all-to-all(bf16[32,8,576]{2,1,0:T(8,128)(2,1)S(1)} %get-tuple-element.13), channel_id=1, replica_groups=mesh['section'=4,'group'=4,'head'=8] {'section','head'}, dimensions={0} | all-to-all | bytes 589824 | tf_op jit(solution)/shard_map/all_to_all | solution.py:26
  22.0 0.0 collective-permute-done.k1
  22.0 0.0 collective-permute-done.1.k2
  22.0 0.0 collective-permute-done.2.k3
  22.0 0.0 copy-start
  22.0 0.0 copy-start.4
  22.0 0.0 copy-start.5
  22.0 1.1 %shard_map.110 = bf16[256,640]{1,0:T(8,128)(2,1)S(1)} custom-call(bf16[256,576]{1,0:T(8,128)(2,1)S(1)} %bitcast.12, s32[1,8]{1,0:T(1,128)S(1)} %get-tuple-element.14.length_ref, bf16[2,576,128]{2,1,0:T(8,128)(2,1)S(1)} %get-tuple-element.15.k0, bf16[2,576,128]{2,1,0:T(8,128)(2,1)S(1)} %collective-permute-done.k1, ...), custom_call_target="tpu_custom_call" | custom-call | tf_op jit(solution)/shard_map/pallas_call | solution.py:288
  23.1 12.2 %all_to_all.46 = bf16[32,8,640]{2,1,0:T(8,128)(2,1)S(1)} all-to-all(bf16[32,8,640]{2,1,0:T(8,128)(2,1)S(1)} %bitcast.13), channel_id=1, replica_groups=mesh['section'=4,'group'=4,'head'=8] {'section','head'}, dimensions={0} | all-to-all | bytes 655360 | tf_op jit(solution)/shard_map/all_to_all | solution.py:26
  35.3 0.0 copy-done
  35.3 0.0 copy-done.4
  35.3 0.0 copy-done.5
  35.3 0.0 copy-start.6
  35.3 0.0 copy-start.7
  35.3 0.0 copy-start.1
  35.3 0.0 copy-start.2
  35.4 1.4 %shard_map.111 = bf16[4,8,8,896]{3,2,1,0:T(8,128)(2,1)S(1)} custom-call(bf16[256,640]{1,0:T(8,128)(2,1)S(1)} %bitcast.14, bf16[4,512,128]{2,1,0:T(8,128)(2,1)S(1)} %copy-done.4, bf16[512,7168]{1,0:T(8,128)(2,1)S(1)} %copy-done, bf16[1,2,896]{2,1,0:T(2,128)(2,1)S(1)} %copy-done.5, bf16[1,896,2048]{2,1,0:T(8,128)(2,1)} %gate_ref.1, bf16[1,896,2048]{2,1,0:T(8,128)(2,1)} %up_ref.1), custom_call_target="tpu_custom_call" | custom-call | tf_op jit(solution)/shard_map/pallas_call | solution.py:288
  36.8 13.1 %all_to_all.47 = bf16[32,8,896]{2,1,0:T(8,128)(2,1)S(1)} all-to-all(bf16[32,8,896]{2,1,0:T(8,128)(2,1)S(1)} %bitcast.11), channel_id=1, replica_groups=mesh['section'=4,'group'=4,'head'=8] {'section','head'}, dimensions={0} | all-to-all | bytes 917504 | tf_op jit(solution)/shard_map/all_to_all | solution.py:26
  49.9 0.1 shard_map.112.hidden_ref.r0
  50.0 7.8 %collective-permute-start.5 = (bf16[8,896]{1,0:T(8,128)(2,1)S(1)}, bf16[8,896]{1,0:T(8,128)(2,1)S(1)}, u32[]{:S(2)}, u32[]{:S(2)}) collective-permute-start(bf16[8,896]{1,0:T(8,128)(2,1)S(1)} %shard_map.112.hidden_ref.r0), channel_id=1, source_target_pairs={{0,24},{8,16},{16,8},{24,0},{1,25},{9,17},{17,9},{25,1},{2,26},{10... | collective-permute-start | bytes 43016 | tf_op jit(solution)/shard_map/ppermute | solution.py:363
  57.7 0.3 collective-permute-start.4
  58.1 0.1 collective-permute-start.3
  58.2 0.0 copy-done.6
  58.2 0.0 copy-done.7
  58.2 0.2 shard_map.113
  58.4 1.1 %collective-permute-done.5.r3 = bf16[8,896]{1,0:T(8,128)(2,1)S(1)} collective-permute-done((bf16[8,896]{1,0:T(8,128)(2,1)S(1)}, bf16[8,896]{1,0:T(8,128)(2,1)S(1)}, u32[]{:S(2)}, u32[]{:S(2)}) %collective-permute-start.5) | collective-permute-done | bytes 14368 | tf_op jit(solution)/shard_map/ppermute | solution.py:363
  59.5 2.3 %collective-permute-done.4.r2 = bf16[8,896]{1,0:T(8,128)(2,1)S(1)} collective-permute-done((bf16[8,896]{1,0:T(8,128)(2,1)S(1)}, bf16[8,896]{1,0:T(8,128)(2,1)S(1)}, u32[]{:S(2)}, u32[]{:S(2)}) %collective-permute-start.4) | collective-permute-done | bytes 14368 | tf_op jit(solution)/shard_map/ppermute | solution.py:363
  61.8 0.0 collective-permute-done.3.r1
  61.8 0.0 copy-done.1
  61.8 0.0 copy-done.2
  61.8 0.0 copy-start.3
  61.8 1.4 %shard_map.114 = bf16[8,136,128]{2,1,0:T(8,128)(2,1)S(1)} custom-call(bf16[8,896]{1,0:T(8,128)(2,1)S(1)} %shard_map.112.hidden_ref.r0, bf16[8,896]{1,0:T(8,128)(2,1)S(1)} %collective-permute-done.3.r1, bf16[8,896]{1,0:T(8,128)(2,1)S(1)} %collective-permute-done.4.r2, bf16[8,896]{1,0:T(8,128)(2,1)S(1)} %collective-permute-done.5.r3, ...), custom_call_target="tpu_custom_call" | custom-call | tf_op jit(solution)/shard_map/pallas_call | solution.py:288
  63.2 9.6 %all_to_all.48.both_ref = bf16[8,136,128]{2,1,0:T(8,128)(2,1)S(1)} all-to-all(bf16[8,136,128]{2,1,0:T(8,128)(2,1)S(1)} %shard_map.114), channel_id=1, replica_groups=mesh['section'=4,'group'=4,'head'=8] {'head'}, dimensions={0} | all-to-all | bytes 557056 | tf_op jit(solution)/shard_map/all_to_all | solution.py:26
  72.8 0.1 shard_map.115
  73.0 7.9 %all_to_all.49.act_ref = bf16[8,32,256]{2,1,0:T(8,128)(2,1)S(1)} all-to-all(bf16[8,32,256]{2,1,0:T(8,128)(2,1)S(1)} %shard_map.115), channel_id=1, replica_groups=mesh['section'=4,'group'=4,'head'=8] {'head'}, dimensions={0} | all-to-all | bytes 262144 | tf_op jit(solution)/shard_map/all_to_all | solution.py:26
  80.9 0.0 copy-done.3
  80.9 0.7 shard_map.116
  81.6 12.6 %all_to_all.50.back_ref = bf16[16,2,896]{2,1,0:T(2,128)(2,1)S(1)} all-to-all(bf16[16,2,896]{2,1,0:T(2,128)(2,1)S(1)} %shard_map.116), channel_id=1, replica_groups=mesh['section'=4,'group'=4,'head'=8] {'section','group'}, dimensions={0} | all-to-all | bytes 114688 | tf_op jit(solution)/shard_map/all_to_all | solution.py:26
  94.3 0.7 shard_map.117
Async XLA Ops:
  1.3 20.7 %collective-permute-start = (bf16[2,576,128]{2,1,0:T(8,128)(2,1)S(1)}, bf16[2,576,128]{2,1,0:T(8,128)(2,1)S(1)}, u32[]{:S(2)}, u32[]{:S(2)}) collective-permute-start(bf16[2,576,128]{2,1,0:T(8,128)(2,1)S(1)} %get-tuple-element.16), channel_id=1, source_target_pairs={{0,32},{1,33},{2,34},{3,35},{4,36},{5,37},{6,38},{7,39},{32,64},{3... | collective-permute-start | bytes 884744 | tf_op jit(solution)/shard_map/ppermute | solution.py:322
  3.4 18.6 %collective-permute-start.1 = (bf16[2,576,128]{2,1,0:T(8,128)(2,1)S(1)}, bf16[2,576,128]{2,1,0:T(8,128)(2,1)S(1)}, u32[]{:S(2)}, u32[]{:S(2)}) collective-permute-start(bf16[2,576,128]{2,1,0:T(8,128)(2,1)S(1)} %get-tuple-element.17), channel_id=1, source_target_pairs={{0,2},{1,3},{2,4},{3,5},{4,6},{5,7},{6,0},{7,1},{32,34},{33,35},{3... | collective-permute-start | bytes 884744 | tf_op jit(solution)/shard_map/ppermute | solution.py:322
  5.1 16.9 %collective-permute-start.2 = (bf16[2,576,128]{2,1,0:T(8,128)(2,1)S(1)}, bf16[2,576,128]{2,1,0:T(8,128)(2,1)S(1)}, u32[]{:S(2)}, u32[]{:S(2)}) collective-permute-start(bf16[2,576,128]{2,1,0:T(8,128)(2,1)S(1)} %get-tuple-element.18), channel_id=1, source_target_pairs={{0,102},{1,103},{2,96},{3,97},{4,98},{5,99},{6,100},{7,101},{32,6}... | collective-permute-start | bytes 884744 | tf_op jit(solution)/shard_map/ppermute | solution.py:322
  22.0 13.3 %copy-start = (bf16[512,7168]{1,0:T(8,128)(2,1)S(1)}, bf16[512,7168]{1,0:T(8,128)(2,1)}, u32[]{:S(2)}) copy-start(bf16[512,7168]{1,0:T(8,128)(2,1)} %out_w_ref.1) | copy-start | bytes 22020100
  22.0 13.3 %copy-start.4 = (bf16[4,512,128]{2,1,0:T(8,128)(2,1)S(1)}, bf16[4,512,128]{2,1,0:T(8,128)(2,1)}, u32[]{:S(2)}) copy-start(bf16[4,512,128]{2,1,0:T(8,128)(2,1)} %uv_ref.1) | copy-start | bytes 1572868
  22.0 13.3 %copy-start.5 = (bf16[1,2,896]{2,1,0:T(2,128)(2,1)S(1)}, bf16[1,2,896]{2,1,0:T(2,128)(2,1)}, u32[]{:S(2)}) copy-start(bf16[1,2,896]{2,1,0:T(2,128)(2,1)} %resid_ref.1) | copy-start | bytes 10756
  35.3 22.9 %copy-start.6 = (s32[1,2,8]{2,1,0:T(2,128)S(1)}, s32[1,2,8]{2,1,0:T(2,128)}, u32[]{:S(2)}) copy-start(s32[1,2,8]{2,1,0:T(2,128)} %picks_ref.1) | copy-start | bytes 196
  35.3 22.9 %copy-start.7 = (f32[1,2,8]{2,1,0:T(2,128)S(1)}, f32[1,2,8]{2,1,0:T(2,128)}, u32[]{:S(2)}) copy-start(f32[1,2,8]{2,1,0:T(2,128)} %logits_ref.1) | copy-start | bytes 196
  35.3 26.5 %copy-start.1 = (bf16[1,896,2048]{2,1,0:T(8,128)(2,1)S(1)}, bf16[1,896,2048]{2,1,0:T(8,128)(2,1)}, u32[]{:S(2)}) copy-start(bf16[1,896,2048]{2,1,0:T(8,128)(2,1)} %gate_ref.1) | copy-start | bytes 11010052
  35.3 26.5 %copy-start.2 = (bf16[1,896,2048]{2,1,0:T(8,128)(2,1)S(1)}, bf16[1,896,2048]{2,1,0:T(8,128)(2,1)}, u32[]{:S(2)}) copy-start(bf16[1,896,2048]{2,1,0:T(8,128)(2,1)} %up_ref.1) | copy-start | bytes 11010052
  50.0 9.6 %collective-permute-start.5 = (bf16[8,896]{1,0:T(8,128)(2,1)S(1)}, bf16[8,896]{1,0:T(8,128)(2,1)S(1)}, u32[]{:S(2)}, u32[]{:S(2)}) collective-permute-start(bf16[8,896]{1,0:T(8,128)(2,1)S(1)} %shard_map.112.hidden_ref.r0), channel_id=1, source_target_pairs={{0,24},{8,16},{16,8},{24,0},{1,25},{9,17},{17,9},{25,1},{2,26},{10... | collective-permute-start | bytes 43016 | tf_op jit(solution)/shard_map/ppermute | solution.py:363
  57.7 4.1 %collective-permute-start.4 = (bf16[8,896]{1,0:T(8,128)(2,1)S(1)}, bf16[8,896]{1,0:T(8,128)(2,1)S(1)}, u32[]{:S(2)}, u32[]{:S(2)}) collective-permute-start(bf16[8,896]{1,0:T(8,128)(2,1)S(1)} %shard_map.112.hidden_ref.r0), channel_id=1, source_target_pairs={{0,16},{8,24},{16,0},{24,8},{1,17},{9,25},{17,1},{25,9},{2,18},{10... | collective-permute-start | bytes 43016 | tf_op jit(solution)/shard_map/ppermute | solution.py:363
  58.1 3.7 %collective-permute-start.3 = (bf16[8,896]{1,0:T(8,128)(2,1)S(1)}, bf16[8,896]{1,0:T(8,128)(2,1)S(1)}, u32[]{:S(2)}, u32[]{:S(2)}) collective-permute-start(bf16[8,896]{1,0:T(8,128)(2,1)S(1)} %shard_map.112.hidden_ref.r0), channel_id=1, source_target_pairs={{0,8},{8,0},{16,24},{24,16},{1,9},{9,1},{17,25},{25,17},{2,10},{10... | collective-permute-start | bytes 43016 | tf_op jit(solution)/shard_map/ppermute | solution.py:363
  61.8 19.1 %copy-start.3 = (bf16[1,2048,896]{2,1,0:T(8,128)(2,1)S(1)}, bf16[1,2048,896]{2,1,0:T(8,128)(2,1)}, u32[]{:S(2)}) copy-start(bf16[1,2048,896]{2,1,0:T(8,128)(2,1)} %down_ref.1) | copy-start | bytes 11010052

commit v4 on v3

--- a/solution.py
+++ b/solution.py
@@ -225,13 +225,26 @@
     row = lax.broadcasted_iota(jnp.int32, (8, 128), 0)
     low = jnp.where(row == 2, squares - high - middle, 0.0)
     squares = jnp.where(row == 0, high, jnp.where(row == 1, middle, low))
+    count, cut = rows.shape[0], rows.shape[1] - 128
+    none = jnp.zeros((count, 128), f32)
+    last = wide[:, cut:]
+    tail = jnp.concatenate(
+        [
+            jnp.concatenate([last, none], axis=1),
+            jnp.concatenate([none, last], axis=1),
+        ],
+        axis=0,
+    ).astype(bf16)
     n_head = both_ref.shape[0]
     ff = gate_ref.shape[2] // n_head
     for k in range(n_head):
         columns = slice(k * ff, (k + 1) * ff)
         parts = []
-        for w in (gate_ref, up_ref):
-            sums = contract(rows, w[0, :, columns], ((1,), (0,)))
+        ends = [w[0, cut:, columns] for w in (gate_ref, up_ref)]
+        ends = contract(tail, jnp.concatenate(ends, axis=0), ((1,), (0,)))
+        for i, w in enumerate((gate_ref, up_ref)):
+            sums = contract(rows[:, :cut], w[0, :cut, columns], ((1,), (0,)))
+            sums += ends[i * count : (i + 1) * count]
             parts += [sums[:, c : c + 128] for c in range(0, ff, 128)]
         both_ref[k] = jnp.concatenate(parts + [squares], axis=0).astype(bf16)
 

time: 95.3 us -> 95.2 us (level)
  no operation moved by 1% of the time
where the time goes in v4:
time: 95.2 us; the launch traced here: 94.9 us
  blocking collectives  69.1 us (73%)
  starting transfers between devices  15.3 us (16%)
  Pallas kernels  6.93 us (7%)
  waiting for transfers between devices  3.4 us (4%)
    all_to_all x6, blocking collectives, exchange(): return lax.all_to_all(x, axes, split_axis=0, concat_axis=0, tiled=True)  69.1 us
    ppermute x3, starting transfers between devices, from_group(): return lax.ppermute(hidden, 'group', [(g, g ^ d) for g in range(n_group)])  8.28 us
    ppermute x3, starting transfers between devices, passed(): return lax.ppermute(part, SPLIT, pairs)  7.05 us
    pallas_call x9, Pallas kernels, run(): pl.pallas_call(kernel, out_shape=shapes[0] if single else shapes, in_spec...  6.93 us
    ppermute x3, waiting for transfers between devices, from_group(): return lax.ppermute(hidden, 'group', [(g, g ^ d) for g in range(n_group)])  3.39 us
  transfers between devices with their start and end apart: 6, of which 2 were waited for; matrix products, arithmetic and copies ran while one was open for 0% of the time, Pallas kernels for 0%

profile of v4, /device:TPU:1, one launch (start us, length us, event | category | flops | bytes accessed | tf_op | source)
XLA Modules:
  0.0 94.9 jit_solution(5638111299456236033)
XLA Ops:
  0.0 1.3 %shard_map.109 = (bf16[32,8,576]{2,1,0:T(8,128)(2,1)S(1)}, bf16[2,576,128]{2,1,0:T(8,128)(2,1)S(1)}, bf16[2,576,128]{2,1,0:T(8,128)(2,1)S(1)}, bf16[2,576,128]{2...) custom-call(bf16[1,8,4,576]{3,2,1,0:T(4,128)(2,1)} %queries_ref.1, ...), custom_call_target="tpu_custom_call" | custom-call | tf_op jit(solution)/shard_map/pallas_call | solution.py:301
  1.3 2.1 %collective-permute-start = (bf16[2,576,128]{2,1,0:T(8,128)(2,1)S(1)}, bf16[2,576,128]{2,1,0:T(8,128)(2,1)S(1)}, u32[]{:S(2)}, u32[]{:S(2)}) collective-permute-start(bf16[2,576,128]{2,1,0:T(8,128)(2,1)S(1)} %get-tuple-element.16), channel_id=1, source_target_pairs={{0,32},{1,33},{2,34},{3,35},{4,36},{5,37},{6,38},{7,39},{32,64},{3... | collective-permute-start | bytes 884744 | tf_op jit(solution)/shard_map/ppermute | solution.py:335
  3.4 1.6 %collective-permute-start.1 = (bf16[2,576,128]{2,1,0:T(8,128)(2,1)S(1)}, bf16[2,576,128]{2,1,0:T(8,128)(2,1)S(1)}, u32[]{:S(2)}, u32[]{:S(2)}) collective-permute-start(bf16[2,576,128]{2,1,0:T(8,128)(2,1)S(1)} %get-tuple-element.17), channel_id=1, source_target_pairs={{0,2},{1,3},{2,4},{3,5},{4,6},{5,7},{6,0},{7,1},{32,34},{33,35},{3... | collective-permute-start | bytes 884744 | tf_op jit(solution)/shard_map/ppermute | solution.py:335
  5.1 3.3 %collective-permute-start.2 = (bf16[2,576,128]{2,1,0:T(8,128)(2,1)S(1)}, bf16[2,576,128]{2,1,0:T(8,128)(2,1)S(1)}, u32[]{:S(2)}, u32[]{:S(2)}) collective-permute-start(bf16[2,576,128]{2,1,0:T(8,128)(2,1)S(1)} %get-tuple-element.18), channel_id=1, source_target_pairs={{0,102},{1,103},{2,96},{3,97},{4,98},{5,99},{6,100},{7,101},{32,6}... | collective-permute-start | bytes 884744 | tf_op jit(solution)/shard_map/ppermute | solution.py:335
  8.4 13.6 %all_to_all.45 = bf16[32,8,576]{2,1,0:T(8,128)(2,1)S(1)} all-to-all(bf16[32,8,576]{2,1,0:T(8,128)(2,1)S(1)} %get-tuple-element.13), channel_id=1, replica_groups=mesh['section'=4,'group'=4,'head'=8] {'section','head'}, dimensions={0} | all-to-all | bytes 589824 | tf_op jit(solution)/shard_map/all_to_all | solution.py:26
  22.0 0.0 collective-permute-done.k1
  22.0 0.0 collective-permute-done.1.k2
  22.0 0.0 collective-permute-done.2.k3
  22.0 0.0 copy-start
  22.0 0.0 copy-start.4
  22.0 0.0 copy-start.5
  22.0 1.1 %shard_map.110 = bf16[256,640]{1,0:T(8,128)(2,1)S(1)} custom-call(bf16[256,576]{1,0:T(8,128)(2,1)S(1)} %bitcast.12, s32[1,8]{1,0:T(1,128)S(1)} %get-tuple-element.14.length_ref, bf16[2,576,128]{2,1,0:T(8,128)(2,1)S(1)} %get-tuple-element.15.k0, bf16[2,576,128]{2,1,0:T(8,128)(2,1)S(1)} %collective-permute-done.k1, ...), custom_call_target="tpu_custom_call" | custom-call | tf_op jit(solution)/shard_map/pallas_call | solution.py:301
  23.1 12.2 %all_to_all.46 = bf16[32,8,640]{2,1,0:T(8,128)(2,1)S(1)} all-to-all(bf16[32,8,640]{2,1,0:T(8,128)(2,1)S(1)} %bitcast.13), channel_id=1, replica_groups=mesh['section'=4,'group'=4,'head'=8] {'section','head'}, dimensions={0} | all-to-all | bytes 655360 | tf_op jit(solution)/shard_map/all_to_all | solution.py:26
  35.3 0.0 copy-done
  35.3 0.0 copy-done.4
  35.3 0.0 copy-done.5
  35.3 0.0 copy-start.6
  35.3 0.0 copy-start.7
  35.3 0.0 copy-start.1
  35.3 0.0 copy-start.2
  35.4 1.4 %shard_map.111 = bf16[4,8,8,896]{3,2,1,0:T(8,128)(2,1)S(1)} custom-call(bf16[256,640]{1,0:T(8,128)(2,1)S(1)} %bitcast.14, bf16[4,512,128]{2,1,0:T(8,128)(2,1)S(1)} %copy-done.4, bf16[512,7168]{1,0:T(8,128)(2,1)S(1)} %copy-done, bf16[1,2,896]{2,1,0:T(2,128)(2,1)S(1)} %copy-done.5, bf16[1,896,2048]{2,1,0:T(8,128)(2,1)} %gate_ref.1, bf16[1,896,2048]{2,1,0:T(8,128)(2,1)} %up_ref.1), custom_call_target="tpu_custom_call" | custom-call | tf_op jit(solution)/shard_map/pallas_call | solution.py:301
  36.8 13.1 %all_to_all.47 = bf16[32,8,896]{2,1,0:T(8,128)(2,1)S(1)} all-to-all(bf16[32,8,896]{2,1,0:T(8,128)(2,1)S(1)} %bitcast.11), channel_id=1, replica_groups=mesh['section'=4,'group'=4,'head'=8] {'section','head'}, dimensions={0} | all-to-all | bytes 917504 | tf_op jit(solution)/shard_map/all_to_all | solution.py:26
  49.9 0.1 shard_map.112.hidden_ref.r0
  50.0 7.8 %collective-permute-start.5 = (bf16[8,896]{1,0:T(8,128)(2,1)S(1)}, bf16[8,896]{1,0:T(8,128)(2,1)S(1)}, u32[]{:S(2)}, u32[]{:S(2)}) collective-permute-start(bf16[8,896]{1,0:T(8,128)(2,1)S(1)} %shard_map.112.hidden_ref.r0), channel_id=1, source_target_pairs={{0,24},{8,16},{16,8},{24,0},{1,25},{9,17},{17,9},{25,1},{2,26},{10... | collective-permute-start | bytes 43016 | tf_op jit(solution)/shard_map/ppermute | solution.py:376
  57.7 0.3 collective-permute-start.4
  58.1 0.1 collective-permute-start.3
  58.2 0.0 copy-done.6
  58.2 0.0 copy-done.7
  58.2 0.2 shard_map.113
  58.4 1.1 %collective-permute-done.5.r3 = bf16[8,896]{1,0:T(8,128)(2,1)S(1)} collective-permute-done((bf16[8,896]{1,0:T(8,128)(2,1)S(1)}, bf16[8,896]{1,0:T(8,128)(2,1)S(1)}, u32[]{:S(2)}, u32[]{:S(2)}) %collective-permute-start.5) | collective-permute-done | bytes 14368 | tf_op jit(solution)/shard_map/ppermute | solution.py:376
  59.5 2.3 %collective-permute-done.4.r2 = bf16[8,896]{1,0:T(8,128)(2,1)S(1)} collective-permute-done((bf16[8,896]{1,0:T(8,128)(2,1)S(1)}, bf16[8,896]{1,0:T(8,128)(2,1)S(1)}, u32[]{:S(2)}, u32[]{:S(2)}) %collective-permute-start.4) | collective-permute-done | bytes 14368 | tf_op jit(solution)/shard_map/ppermute | solution.py:376
  61.8 0.0 collective-permute-done.3.r1
  61.8 0.0 copy-done.1
  61.8 0.0 copy-done.2
  61.8 0.0 copy-start.3
  61.8 1.3 %shard_map.114 = bf16[8,136,128]{2,1,0:T(8,128)(2,1)S(1)} custom-call(bf16[8,896]{1,0:T(8,128)(2,1)S(1)} %shard_map.112.hidden_ref.r0, bf16[8,896]{1,0:T(8,128)(2,1)S(1)} %collective-permute-done.3.r1, bf16[8,896]{1,0:T(8,128)(2,1)S(1)} %collective-permute-done.4.r2, bf16[8,896]{1,0:T(8,128)(2,1)S(1)} %collective-permute-done.5.r3, ...), custom_call_target="tpu_custom_call" | custom-call | tf_op jit(solution)/shard_map/pallas_call | solution.py:301
  63.2 9.6 %all_to_all.48.both_ref = bf16[8,136,128]{2,1,0:T(8,128)(2,1)S(1)} all-to-all(bf16[8,136,128]{2,1,0:T(8,128)(2,1)S(1)} %shard_map.114), channel_id=1, replica_groups=mesh['section'=4,'group'=4,'head'=8] {'head'}, dimensions={0} | all-to-all | bytes 557056 | tf_op jit(solution)/shard_map/all_to_all | solution.py:26
  72.8 0.1 shard_map.115
  72.9 7.9 %all_to_all.49.act_ref = bf16[8,32,256]{2,1,0:T(8,128)(2,1)S(1)} all-to-all(bf16[8,32,256]{2,1,0:T(8,128)(2,1)S(1)} %shard_map.115), channel_id=1, replica_groups=mesh['section'=4,'group'=4,'head'=8] {'head'}, dimensions={0} | all-to-all | bytes 262144 | tf_op jit(solution)/shard_map/all_to_all | solution.py:26
  80.9 0.0 copy-done.3
  80.9 0.7 shard_map.116
  81.6 12.6 %all_to_all.50.back_ref = bf16[16,2,896]{2,1,0:T(2,128)(2,1)S(1)} all-to-all(bf16[16,2,896]{2,1,0:T(2,128)(2,1)S(1)} %shard_map.116), channel_id=1, replica_groups=mesh['section'=4,'group'=4,'head'=8] {'section','group'}, dimensions={0} | all-to-all | bytes 114688 | tf_op jit(solution)/shard_map/all_to_all | solution.py:26
  94.2 0.7 shard_map.117
Async XLA Ops:
  1.3 20.7 %collective-permute-start = (bf16[2,576,128]{2,1,0:T(8,128)(2,1)S(1)}, bf16[2,576,128]{2,1,0:T(8,128)(2,1)S(1)}, u32[]{:S(2)}, u32[]{:S(2)}) collective-permute-start(bf16[2,576,128]{2,1,0:T(8,128)(2,1)S(1)} %get-tuple-element.16), channel_id=1, source_target_pairs={{0,32},{1,33},{2,34},{3,35},{4,36},{5,37},{6,38},{7,39},{32,64},{3... | collective-permute-start | bytes 884744 | tf_op jit(solution)/shard_map/ppermute | solution.py:335
  3.4 18.6 %collective-permute-start.1 = (bf16[2,576,128]{2,1,0:T(8,128)(2,1)S(1)}, bf16[2,576,128]{2,1,0:T(8,128)(2,1)S(1)}, u32[]{:S(2)}, u32[]{:S(2)}) collective-permute-start(bf16[2,576,128]{2,1,0:T(8,128)(2,1)S(1)} %get-tuple-element.17), channel_id=1, source_target_pairs={{0,2},{1,3},{2,4},{3,5},{4,6},{5,7},{6,0},{7,1},{32,34},{33,35},{3... | collective-permute-start | bytes 884744 | tf_op jit(solution)/shard_map/ppermute | solution.py:335
  5.1 16.9 %collective-permute-start.2 = (bf16[2,576,128]{2,1,0:T(8,128)(2,1)S(1)}, bf16[2,576,128]{2,1,0:T(8,128)(2,1)S(1)}, u32[]{:S(2)}, u32[]{:S(2)}) collective-permute-start(bf16[2,576,128]{2,1,0:T(8,128)(2,1)S(1)} %get-tuple-element.18), channel_id=1, source_target_pairs={{0,102},{1,103},{2,96},{3,97},{4,98},{5,99},{6,100},{7,101},{32,6}... | collective-permute-start | bytes 884744 | tf_op jit(solution)/shard_map/ppermute | solution.py:335
  22.0 13.3 %copy-start = (bf16[512,7168]{1,0:T(8,128)(2,1)S(1)}, bf16[512,7168]{1,0:T(8,128)(2,1)}, u32[]{:S(2)}) copy-start(bf16[512,7168]{1,0:T(8,128)(2,1)} %out_w_ref.1) | copy-start | bytes 22020100
  22.0 13.3 %copy-start.4 = (bf16[4,512,128]{2,1,0:T(8,128)(2,1)S(1)}, bf16[4,512,128]{2,1,0:T(8,128)(2,1)}, u32[]{:S(2)}) copy-start(bf16[4,512,128]{2,1,0:T(8,128)(2,1)} %uv_ref.1) | copy-start | bytes 1572868
  22.0 13.3 %copy-start.5 = (bf16[1,2,896]{2,1,0:T(2,128)(2,1)S(1)}, bf16[1,2,896]{2,1,0:T(2,128)(2,1)}, u32[]{:S(2)}) copy-start(bf16[1,2,896]{2,1,0:T(2,128)(2,1)} %resid_ref.1) | copy-start | bytes 10756
  35.3 22.9 %copy-start.6 = (s32[1,2,8]{2,1,0:T(2,128)S(1)}, s32[1,2,8]{2,1,0:T(2,128)}, u32[]{:S(2)}) copy-start(s32[1,2,8]{2,1,0:T(2,128)} %picks_ref.1) | copy-start | bytes 196
  35.3 22.9 %copy-start.7 = (f32[1,2,8]{2,1,0:T(2,128)S(1)}, f32[1,2,8]{2,1,0:T(2,128)}, u32[]{:S(2)}) copy-start(f32[1,2,8]{2,1,0:T(2,128)} %logits_ref.1) | copy-start | bytes 196
  35.3 26.5 %copy-start.1 = (bf16[1,896,2048]{2,1,0:T(8,128)(2,1)S(1)}, bf16[1,896,2048]{2,1,0:T(8,128)(2,1)}, u32[]{:S(2)}) copy-start(bf16[1,896,2048]{2,1,0:T(8,128)(2,1)} %gate_ref.1) | copy-start | bytes 11010052
  35.3 26.5 %copy-start.2 = (bf16[1,896,2048]{2,1,0:T(8,128)(2,1)S(1)}, bf16[1,896,2048]{2,1,0:T(8,128)(2,1)}, u32[]{:S(2)}) copy-start(bf16[1,896,2048]{2,1,0:T(8,128)(2,1)} %up_ref.1) | copy-start | bytes 11010052
  50.0 9.6 %collective-permute-start.5 = (bf16[8,896]{1,0:T(8,128)(2,1)S(1)}, bf16[8,896]{1,0:T(8,128)(2,1)S(1)}, u32[]{:S(2)}, u32[]{:S(2)}) collective-permute-start(bf16[8,896]{1,0:T(8,128)(2,1)S(1)} %shard_map.112.hidden_ref.r0), channel_id=1, source_target_pairs={{0,24},{8,16},{16,8},{24,0},{1,25},{9,17},{17,9},{25,1},{2,26},{10... | collective-permute-start | bytes 43016 | tf_op jit(solution)/shard_map/ppermute | solution.py:376
  57.7 4.1 %collective-permute-start.4 = (bf16[8,896]{1,0:T(8,128)(2,1)S(1)}, bf16[8,896]{1,0:T(8,128)(2,1)S(1)}, u32[]{:S(2)}, u32[]{:S(2)}) collective-permute-start(bf16[8,896]{1,0:T(8,128)(2,1)S(1)} %shard_map.112.hidden_ref.r0), channel_id=1, source_target_pairs={{0,16},{8,24},{16,0},{24,8},{1,17},{9,25},{17,1},{25,9},{2,18},{10... | collective-permute-start | bytes 43016 | tf_op jit(solution)/shard_map/ppermute | solution.py:376
  58.1 3.7 %collective-permute-start.3 = (bf16[8,896]{1,0:T(8,128)(2,1)S(1)}, bf16[8,896]{1,0:T(8,128)(2,1)S(1)}, u32[]{:S(2)}, u32[]{:S(2)}) collective-permute-start(bf16[8,896]{1,0:T(8,128)(2,1)S(1)} %shard_map.112.hidden_ref.r0), channel_id=1, source_target_pairs={{0,8},{8,0},{16,24},{24,16},{1,9},{9,1},{17,25},{25,17},{2,10},{10... | collective-permute-start | bytes 43016 | tf_op jit(solution)/shard_map/ppermute | solution.py:376
  61.8 19.0 %copy-start.3 = (bf16[1,2048,896]{2,1,0:T(8,128)(2,1)S(1)}, bf16[1,2048,896]{2,1,0:T(8,128)(2,1)}, u32[]{:S(2)}) copy-start(bf16[1,2048,896]{2,1,0:T(8,128)(2,1)} %down_ref.1) | copy-start | bytes 11010052
